TPU v7x, 256 devices: a whole 4x4x8 slice. The times are simulated.
256 devices in a mesh: ctx: 16 (over y_hi, z), exp: 8 (over x, core), dp: 2 (over y_lo).
Axes of the slice: x: 4, y: 4 (y_hi: 2, y_lo: 2; y = y_hi * 2 + y_lo), z: 8, core: 2. Of those that a mesh axis runs over, the one named last changes fastest.
Arguments:
- residual: bfloat16 [4096, 4096], P(('dp', 'ctx', 'exp')), parts along dimension 0, may hold values from -0.59765625 to 0.59765625
- encoded_query_rows: bfloat16 [4096, 4096], P(('dp', 'ctx'), 'exp'), parts along dimension 0, may hold values from -256 to 256
- quantized_key_rows: bfloat16 [4096, 512], P(('dp', 'ctx')), parts along dimension 0, may hold values from -8 to 8
- quantized_value_rows: bfloat16 [4096, 512], P(('dp', 'ctx')), parts along dimension 0, may hold values from -6 to 6
- key_block_exponent: int32 [64, 4], P(('dp', 'ctx')), parts along dimension 0, may hold values from -2 to 1
- value_block_exponent: int32 [64, 4], P(('dp', 'ctx')), parts along dimension 0, may hold values from -2 to 1
- block_order: int32 [16], replicated, may hold values from 0 to 15, each once
- out_weight: bfloat16 [4096, 4096], P('exp', 'ctx'), may hold values from -0.09375 to 0.09375
- norm_gain: float32 [4096], replicated, may hold values from 0.1 to 1.9
- expert_ids: int32 [4096, 8], P(('dp', 'ctx', 'exp')), parts along dimension 0, may hold values from 0 to 63, all different within a row; in each aligned block of 16 rows (0 to 15, 16 to 31, ...) at most 3 rows name the same one
- route_weight: float32 [4096, 8], P(('dp', 'ctx', 'exp')), parts along dimension 0, may hold values from 0.05 to 0.25
- gate_weight: bfloat16 [128, 4096, 384], P(('ctx', 'exp')), may hold values from -0.09375 to 0.09375
- gate_scale: int32 [128, 32, 3], P(('ctx', 'exp')), may hold values from -1 to 1
- up_weight: bfloat16 [128, 4096, 384], P(('ctx', 'exp')), may hold values from -0.09375 to 0.09375
- up_scale: int32 [128, 32, 3], P(('ctx', 'exp')), may hold values from -1 to 1
- down_weight: bfloat16 [128, 384, 4096], P(('ctx', 'exp')), may hold values from -0.21875 to 0.21875
- down_scale: int32 [128, 3, 32], P(('ctx', 'exp')), may hold values from -1 to 1
Outputs:
- layer_out: bfloat16 [4096, 4096], P(('dp', 'ctx', 'exp')), parts along dimension 0
There are 2 independent parts, one for each index of `dp`. A program takes and returns all parts, laid end to end along the dimension named above; an argument that names none is the same for every part. Nothing has to cross between parts.
Inputs may be any that keep to these rules, and one draw needn't show every extreme that they name: `expert_ids`: each row names 8 different experts. Among the rows of one device (16 aligned rows), no expert is named by more than 3 rows, a bound that some block reaches. `block_order`: A permutation of the ctx indices.
All inputs are finite; a program needn't handle non-finite values.
Results may differ from a plain program's by a relative error of at most 0.03.
Values may be sent and summed in bfloat16 or wider, within the bound.
A program may use at most 128 MiB of HBM per device.

v0:
```python
import math

import jax
import jax.numpy as jnp
from jax import lax
from jax.sharding import PartitionSpec as P

QUERY_HEADS = 32
KEY_VALUE_HEADS = 4
HEAD_SIZE = 128
TOP = 8
SCALE_POSITIONS = 64


def from_partner(array, axis, bit):
    return lax.ppermute(array, axis, [(i, i ^ 1 << bit) for i in range(lax.axis_size(axis))])


def pow_two(exponent, lowest, highest):
    result_sum = jnp.zeros(exponent.shape, jnp.float32)
    for power_of in range(lowest, highest + 1):
        result_sum = result_sum + jnp.where(exponent == power_of, 2.0**power_of, 0.0)
    return result_sum


def dequant(values, exponents, lowest, highest):
    row_blocks = exponents.shape[-2]
    col_blocks = exponents.shape[-1]
    row_rep = values.shape[-2] // row_blocks
    col_rep = values.shape[-1] // col_blocks
    factor = pow_two(exponents, lowest, highest).astype(jnp.bfloat16)
    shaped = values.reshape(values.shape[:-2] + (row_blocks, row_rep, col_blocks, col_rep))
    return (shaped * factor[..., :, None, :, None]).reshape(values.shape)


def shards(
    residual,
    encoded_query_rows,
    quantized_key_rows,
    quantized_value_rows,
    key_block_exponent,
    value_block_exponent,
    block_order,
    out_weight,
    norm_gain,
    expert_ids,
    route_weight,
    gate_weight,
    gate_scale,
    up_weight,
    up_scale,
    down_weight,
    down_scale,
):
    span_rows = encoded_query_rows.shape[0]
    head_count = encoded_query_rows.shape[1] // HEAD_SIZE
    query_group_width = QUERY_HEADS // KEY_VALUE_HEADS
    ctx_count = lax.axis_size("ctx")
    exp_count = lax.axis_size("exp")
    experts = ctx_count * exp_count // 2
    tok_count = residual.shape[0]
    model_width = residual.shape[1]
    half_width = model_width // 2
    capacity = min(tok_count, max(2, 3 * tok_count * TOP // (2 * experts)))
    my_ctx = lax.axis_index("ctx")
    my_exp = lax.axis_index("exp")
    half_bit = my_exp % 2
    kv_head = my_exp * head_count // query_group_width
    ctx_ids = jnp.arange(ctx_count, dtype=jnp.int32)

    def place_of(block_ids):
        return jnp.sum(
            jnp.where(block_ids[:, None] == ctx_ids[None, :], block_order[None, :], 0), axis=1
        )

    own_place = place_of(jnp.reshape(my_ctx, (1,)))[0]
    query_place = own_place * span_rows + jnp.arange(span_rows, dtype=jnp.int32)

    def head_rows(row_vals, scales):
        picked = lax.dynamic_slice_in_dim(row_vals, kv_head * HEAD_SIZE, HEAD_SIZE, 1)
        factor = lax.dynamic_slice_in_dim(scales, kv_head, 1, 1)
        factor = jnp.repeat(pow_two(factor, -2, 1), SCALE_POSITIONS, axis=0)
        return (picked.astype(jnp.float32) * factor).astype(jnp.bfloat16)

    key_head = head_rows(quantized_key_rows, key_block_exponent)
    value_head = head_rows(quantized_value_rows, value_block_exponent)
    queries = encoded_query_rows.reshape(span_rows, head_count, HEAD_SIZE)
    inv_scale = 1.0 / math.sqrt(HEAD_SIZE)
    initial = (
        jnp.full((head_count, span_rows), -1e30, jnp.float32),
        jnp.zeros((head_count, span_rows), jnp.float32),
        jnp.zeros((span_rows, head_count, HEAD_SIZE), jnp.float32),
    )
    key_piece = lax.all_gather(key_head, "ctx", axis=0, tiled=True)
    value_piece = lax.all_gather(value_head, "ctx", axis=0, tiled=True)
    piece_len = key_piece.shape[0]
    row_ids = jnp.arange(piece_len, dtype=jnp.int32)
    key_place = place_of(row_ids // span_rows) * span_rows + row_ids % span_rows
    seen = jnp.min(key_place) <= jnp.max(query_place)

    def update(state_in):
        run_max, run_sum, run_acc = state_in
        scores = (
            jnp.einsum("qhd,kd->hqk", queries, key_piece, preferred_element_type=jnp.float32)
            * inv_scale
        )
        visible_mask = key_place[None, None, :] <= query_place[None, :, None]
        scores = jnp.where(visible_mask, scores, -1e30)
        new_max = jnp.maximum(run_max, jnp.max(scores, axis=-1))
        weights = jnp.where(visible_mask, jnp.exp(scores - new_max[:, :, None]), 0.0)
        factor = jnp.exp(run_max - new_max)
        run_sum = jnp.sum(weights, axis=-1)
        added = jnp.einsum(
            "hqk,kd->qhd",
            weights.astype(jnp.bfloat16),
            value_piece,
            preferred_element_type=jnp.float32,
        )
        run_acc = added
        return (new_max, run_sum, run_acc)

    def unchanged(state_in):
        return state_in

    run_max, run_sum, run_acc = lax.cond(seen, update, unchanged, initial)
    attended = (
        (run_acc / jnp.transpose(run_sum)[:, :, None])
        .astype(jnp.bfloat16)
        .reshape(span_rows, head_count * HEAD_SIZE)
    )
    partial_rows = jnp.dot(
        attended,
        lax.all_gather(out_weight, "ctx", axis=1, tiled=True),
        preferred_element_type=jnp.float32,
    )
    mixed = lax.psum_scatter(
        partial_rows.astype(jnp.bfloat16), "exp", scatter_dimension=0, tiled=True
    ).astype(jnp.float32)
    state_rows = residual.astype(jnp.float32) + mixed
    mean_sq = jnp.mean(state_rows * state_rows, axis=-1, keepdims=True)
    normed = (state_rows * lax.rsqrt(mean_sq + 1e-06) * norm_gain).astype(jnp.bfloat16)
    flat_ids = expert_ids.reshape(-1)
    onehot = (flat_ids[:, None] == jnp.arange(experts, dtype=jnp.int32)[None, :]).astype(jnp.int32)
    before = jnp.cumsum(onehot, axis=0) - onehot
    slot_ids = jnp.sum(before * onehot, axis=1)
    target = flat_ids * capacity + slot_ids
    owner_token = jnp.arange(flat_ids.shape[0], dtype=jnp.int32) // TOP
    slot_table = jnp.full((experts * capacity,), tok_count, jnp.int32).at[target].set(owner_token)
    padded = jnp.concatenate([normed, jnp.zeros((1, model_width), jnp.bfloat16)], axis=0)
    outgoing = padded[slot_table].reshape(experts, 1, capacity, model_width)
    outgoing = jnp.broadcast_to(outgoing, (experts, 2, capacity, model_width)).reshape(
        2 * experts, capacity, model_width
    )
    gate_deq = dequant(gate_weight[0], gate_scale[0], -1, 1)
    up_deq = dequant(up_weight[0], up_scale[0], -1, 1)
    down_deq = dequant(down_weight[0], down_scale[0], -1, 1)
    arrived = lax.all_to_all(outgoing, ("ctx", "exp"), split_axis=0, concat_axis=0, tiled=True)
    flat_rows = arrived.reshape(-1, model_width)
    gate_act = jnp.dot(flat_rows, gate_deq, preferred_element_type=jnp.float32)
    up_act = jnp.dot(flat_rows, up_deq, preferred_element_type=jnp.float32)
    hidden = (jax.nn.silu(gate_act) * up_act).astype(jnp.bfloat16)
    partial_out = jnp.dot(hidden, down_deq, preferred_element_type=jnp.float32).reshape(
        arrived.shape[0], arrived.shape[1], model_width
    )
    kept_cols = lax.dynamic_slice_in_dim(partial_out, half_bit * half_width, half_width, 2)
    given_cols = lax.dynamic_slice_in_dim(partial_out, (1 - half_bit) * half_width, half_width, 2)
    returned = lax.all_to_all(
        (
            kept_cols
            + from_partner(given_cols.astype(jnp.bfloat16), "exp", 0).astype(given_cols.dtype)
        ).astype(jnp.bfloat16),
        ("ctx", "exp"),
        split_axis=0,
        concat_axis=0,
        tiled=True,
    )
    expert_out = (
        returned.reshape(experts, 2, capacity, half_width)
        .transpose(0, 2, 1, 3)
        .reshape(experts * capacity, model_width)
    )
    picked = expert_out[target].astype(jnp.float32) * route_weight.reshape(-1)[:, None]
    combined = jnp.sum(picked.reshape(tok_count, TOP, model_width), axis=1)
    return (state_rows + combined).astype(jnp.bfloat16)


def solution(mesh):
    return jax.shard_map(
        shards,
        mesh=mesh,
        in_specs=(
            P(("dp", "ctx", "exp"), None),
            P(("dp", "ctx"), "exp"),
            P(("dp", "ctx"), None),
            P(("dp", "ctx"), None),
            P(("dp", "ctx"), None),
            P(("dp", "ctx"), None),
            P(),
            P("exp", "ctx"),
            P(),
            P(("dp", "ctx", "exp"), None),
            P(("dp", "ctx", "exp"), None),
            P(("ctx", "exp"), None, None),
            P(("ctx", "exp"), None, None),
            P(("ctx", "exp"), None, None),
            P(("ctx", "exp"), None, None),
            P(("ctx", "exp"), None, None),
            P(("ctx", "exp"), None, None),
        ),
        out_specs=P(("dp", "ctx", "exp"), None),
        check_vma=False,
    )
```

profile of v0, /device:TPU:1, one launch (start us, length us, event | category | flops | bytes accessed | tf_op | source)
XLA Modules:
  0.0 389.0 jit_solution(6350000020058099644)
XLA Ops:
  6.5 0.7 all-gather.2.cloned.1.call-update
  7.3 0.9 fusion.58
  8.3 0.1 broadcast_in_dim.161
  8.4 0.9 fusion.59
  9.3 0.1 broadcast_in_dim.159
  9.4 1.3 fusion.60
  11.3 0.6 iota_add_fusion
  12.0 0.8 select_reduce_fusion
  12.7 0.6 fusion.65
  14.6 0.8 multiply_convert_fusion.1
  15.5 0.8 multiply_convert_fusion.2
  16.3 42.7 %all_gather.10 = bf16[2048,128]{1,0:T(8,128)(2,1)S(1)} all-gather(bf16[128,128]{1,0:T(8,128)(2,1)S(1)} %multiply_convert_fusion.1), channel_id=1, replica_groups=mesh['ctx'=16,'exp'=8,'dp'=2] {'ctx'}, dimensions={0}, use_global_device_ids=true | all-gather | bytes 557056 | tf_op jit(solution)/shard_map/all_gather | solution.py:95
  59.1 34.0 %all_gather.9 = bf16[2048,128]{1,0:T(8,128)(2,1)S(1)} all-gather(bf16[128,128]{1,0:T(8,128)(2,1)S(1)} %multiply_convert_fusion.2), channel_id=1, replica_groups=mesh['ctx'=16,'exp'=8,'dp'=2] {'ctx'}, dimensions={0}, use_global_device_ids=true | all-gather | bytes 557056 | tf_op jit(solution)/shard_map/all_gather | solution.py:94
  93.1 8.7 %conditional.1 = (f32[4,128]{1,0:T(4,128)S(1)}, f32[128,4,128]{0,2,1:T(8,128)S(1)}) conditional(s32[]{:T(128)} %convert_element_type.74, () %tuple.13, (s32[2048]{0:T(1024)S(1)}, s32[128]{0:T(128)S(1)}, bf16[128,512]{1,0:T(8,128)(2,1)}, bf16[2048,128]{1,0:T(8,128)(2,1)S(1)}, bf16[2048,128]{1,0:T(8,128)(2,1)S(1)}) %tuple.14), branch_computations={%region_4.5_spmd, %region_5.8_spmd} | conditional | flops 550764032 | bytes 32395820 | solution.py:125
  93.1 0.3 broadcast_compare_fusion
  93.4 1.6 fusion
  95.1 1.9 copy-done.1
  97.0 1.3 fusion.6
  98.4 0.1 copy.62
  98.5 3.3 fusion.2
  101.8 17.7 %all-gather.2.cloned.1.call-done = bf16[512,4096]{1,0:T(8,128)(2,1)} async-done(((bf16[512,256]{1,0:T(8,128)(2,1)}), bf16[512,4096]{1,0:T(8,128)(2,1)}) %all-gather.2.cloned.1.call-update) | async-done | bytes 4194320 | tf_op jit(solution)/shard_map/all_gather | solution.py:133
  119.5 3.9 %convolution_convert_fusion = bf16[128,4096]{1,0:T(8,128)(2,1)} fusion(bf16[128,512]{0,1:T(8,128)(2,1)S(1)} %bitcast.90, bf16[512,4096]{1,0:T(8,128)(2,1)} %all-gather.2.cloned.1.call-done), kind=kOutput, calls=%fused_computation.21 | convolution fusion | flops 537395200 | bytes 5373952 | tf_op jit(solution)/shard_map/dot_general | solution.py:131
  123.6 0.1 eq.159
  123.7 0.1 fusion.34
  123.8 0.2 reduce_window_sum.11
  123.9 0.1 copy.52
  124.0 0.1 mul.153
  124.1 0.2 select_reduce_fusion.1
  124.3 1.0 scatter_custom_fusion
  125.3 31.8 %reduce-scatter.2.cloned.1.call-done = bf16[16,4096]{1,0:T(8,128)(2,1)} async-done(((bf16[128,4096]{1,0:T(8,128)(2,1)}), bf16[16,4096]{1,0:T(8,128)(2,1)}) %reduce-scatter.2.cloned.1.call-update) | async-done | bytes 131088 | tf_op jit(solution)/shard_map/reduce_scatter | solution.py:136
  157.1 1.1 multiply_reduce_fusion
  158.2 1.0 multiply_convert_fusion
  159.2 2.7 gather_fusion
  161.9 2.7 broadcast_in_dim.164
  164.7 4.1 %broadcast_in_dim.165 = bf16[64,2,3,4096]{3,2,1,0:T(4,128)(2,1)} broadcast(bf16[64,3,4096]{2,1,0:T(4,128)(2,1)S(1)} %broadcast_in_dim.164), dimensions={0,2,3} | broadcast | bytes 4718592 | tf_op jit(solution)/shard_map/broadcast_in_dim | solution.py:151
  168.8 14.4 %all-to-all-start = ((bf16[128,3,4096]{2,1,0:T(4,128)(2,1)}), bf16[128,3,4096]{2,1,0:T(4,128)(2,1)}, u32[]{:S(2)}, u32[]{:S(2)}) async-start(bf16[128,3,4096]{2,1,0:T(4,128)(2,1)} %bitcast.87), calls=%async_computation.1 | async-start | bytes 8388608 | tf_op jit(solution)/shard_map/all_to_all | solution.py:157
  183.2 0.5 mul.155
  183.7 3.4 mul.156
  187.1 4.8 %copy.54 = bf16[1,4096,384]{1,2,0:T(8,128)(2,1)} copy(bf16[1,4096,384]{2,1,0:T(8,128)(2,1)} %param.30) | data formatting | bytes 6291456 | tf_op args[11]
  191.8 0.5 mul.160
  192.3 3.3 mul.161
  195.7 4.8 %copy.55 = bf16[1,4096,384]{1,2,0:T(8,128)(2,1)} copy(bf16[1,4096,384]{2,1,0:T(8,128)(2,1)} %param.32) | data formatting | bytes 6291456 | tf_op args[13]
  200.5 0.5 mul.165
  200.9 3.4 mul.166
  204.3 78.0 %all-to-all-done = bf16[128,3,4096]{2,1,0:T(4,128)(2,1)} async-done(((bf16[128,3,4096]{2,1,0:T(4,128)(2,1)}), bf16[128,3,4096]{2,1,0:T(4,128)(2,1)}, u32[]{:S(2)}, u32[]{:S(2)}) %all-to-all-start) | async-done | bytes 3145760 | tf_op jit(solution)/shard_map/all_to_all | solution.py:157
  282.4 6.0 %reshape.268 = bf16[384,4096]{1,0:T(8,128)(2,1)S(1)} reshape(bf16[128,3,4096]{2,1,0:T(4,128)(2,1)} %all-to-all-done) | data formatting | bytes 6291456 | tf_op jit(solution)/shard_map/reshape | solution.py:158
  288.4 1.7 copy-done.3
  290.0 4.8 %fusion.21 = f32[384,384]{1,0:T(8,128)S(1)} fusion(bf16[384,4096]{1,0:T(8,128)(2,1)S(1)} %reshape.268, bf16[1,4096,384]{1,2,0:T(8,128)(2,1)} %copy.54, bf16[1,4096,384]{1,2,0:T(8,128)(2,1)} %mul.156), kind=kOutput, calls=%fused_computation.26 | convolution fusion | flops 1209532416 | bytes 10027008 | tf_op jit(solution)/shard_map/dot_general | solution.py:159
  294.8 4.6 %fusion.30 = bf16[384,384]{1,0:T(8,128)(2,1)} fusion(bf16[384,4096]{1,0:T(8,128)(2,1)} %copy-done.3, bf16[1,4096,384]{1,2,0:T(8,128)(2,1)S(1)} %copy-done.5, bf16[1,4096,384]{1,2,0:T(8,128)(2,1)S(1)} %copy-done.4, f32[384,384]{1,0:T(8,128)S(1)} %fusion.21), kind=kOutput, calls=%fused_computation.36 | convolution fusion | flops 1210417152 | bytes 10321920 | tf_op jit(solution)/shard_map/dot_general | solution.py:160
  299.4 1.1 dot_general.23
  300.5 3.7 fusion.17
  304.2 2.7 copy-done
  306.9 0.2 dynamic-slice_convert_fusion
  307.1 0.1 collective-permute-start
  307.2 3.4 collective-permute-done
  310.6 2.4 add_convert_fusion
  313.0 2.7 copy.57
  315.7 5.6 %all-to-all-start.1 = ((bf16[128,3,2048]{2,1,0:T(4,128)(2,1)}), bf16[128,3,2048]{2,1,0:T(4,128)(2,1)S(1)}, u32[]{:S(2)}, u32[]{:S(2)}) async-start(bf16[128,3,2048]{2,1,0:T(4,128)(2,1)} %copy.57), calls=%async_computation.2 | async-start | bytes 4194304 | tf_op jit(solution)/shard_map/all_to_all | solution.py:167
  321.4 55.4 %all-to-all-done.1 = bf16[128,3,2048]{2,1,0:T(4,128)(2,1)S(1)} async-done(((bf16[128,3,2048]{2,1,0:T(4,128)(2,1)}), bf16[128,3,2048]{2,1,0:T(4,128)(2,1)S(1)}, u32[]{:S(2)}, u32[]{:S(2)}) %all-to-all-start.1) | async-done | bytes 1572896 | tf_op jit(solution)/shard_map/all_to_all | solution.py:167
  376.7 2.1 copy.58
  378.8 0.6 copy.67
  379.5 1.2 gather_fusion.1
  380.7 0.8 fusion.26
  381.5 0.7 add_convert_fusion.1
  (50 shorter events, 0.5 us)
Async XLA Ops:
  6.5 113.0 %all-gather.2.cloned.1.call-start = ((), (), s32[]{:S(2)}) async-start(), calls=%async_computation.3 | async-start | bytes 4456448 | tf_op jit(solution)/shard_map/all_gather | solution.py:133
  7.3 149.9 %reduce-scatter.2.cloned.1.call-start = ((), (), s32[]{:S(2)}) async-start(), calls=%async_computation.4 | async-start | bytes 1179648 | tf_op jit(solution)/shard_map/reduce_scatter | solution.py:136
  95.1 2.0 copy-start.1
  119.5 4.0 %copy-start.10 = (s32[16,8]{0,1:T(8,128)S(1)}, s32[16,8]{0,1:T(8,128)}, u32[]{:S(2)}) copy-start(s32[16,8]{0,1:T(8,128)} %param.28) | copy-start | bytes 1540
  119.5 37.6 %copy-start.6 = (bf16[16,4096]{1,0:T(8,128)(2,1)S(1)}, bf16[16,4096]{1,0:T(8,128)(2,1)}, u32[]{:S(2)}) copy-start(bf16[16,4096]{1,0:T(8,128)(2,1)} %param.19) | copy-start | bytes 393220
  119.5 38.7 %copy-start.9 = (f32[4096]{0:T(1024)S(1)}, f32[4096]{0:T(1024)}, u32[]{:S(2)}) copy-start(f32[4096]{0:T(1024)} %param.27) | copy-start | bytes 49156
  168.8 14.4 %copy-start.13 = (s32[1,32,3]{1,0,2:T(1,128)S(1)}, s32[1,32,3]{1,0,2:T(1,128)}, u32[]{:S(2)}) copy-start(s32[1,32,3]{1,0,2:T(1,128)} %param.31) | copy-start | bytes 1156
  168.8 14.4 %copy-start.14 = (s32[1,32,3]{1,0,2:T(1,128)S(1)}, s32[1,32,3]{1,0,2:T(1,128)}, u32[]{:S(2)}) copy-start(s32[1,32,3]{1,0,2:T(1,128)} %param.33) | copy-start | bytes 1156
  168.8 113.6 %all-to-all-start = ((bf16[128,3,4096]{2,1,0:T(4,128)(2,1)}), bf16[128,3,4096]{2,1,0:T(4,128)(2,1)}, u32[]{:S(2)}, u32[]{:S(2)}) async-start(bf16[128,3,4096]{2,1,0:T(4,128)(2,1)} %bitcast.87), calls=%async_computation.1 | async-start | bytes 8388608 | tf_op jit(solution)/shard_map/all_to_all | solution.py:157
  195.7 4.8 %copy-start.12 = (s32[1,3,32]{2,0,1:T(1,128)S(1)}, s32[1,3,32]{2,0,1:T(1,128)}, u32[]{:S(2)}) copy-start(s32[1,3,32]{2,0,1:T(1,128)} %param.35) | copy-start | bytes 1156
  288.3 1.7 copy-start.3
  290.0 4.8 %copy-start.4 = (bf16[1,4096,384]{1,2,0:T(8,128)(2,1)S(1)}, bf16[1,4096,384]{1,2,0:T(8,128)(2,1)}, u32[]{:S(2)}) copy-start(bf16[1,4096,384]{1,2,0:T(8,128)(2,1)} %mul.161) | copy-start | bytes 9437188
  290.0 4.8 %copy-start.5 = (bf16[1,4096,384]{1,2,0:T(8,128)(2,1)S(1)}, bf16[1,4096,384]{1,2,0:T(8,128)(2,1)}, u32[]{:S(2)}) copy-start(bf16[1,4096,384]{1,2,0:T(8,128)(2,1)} %copy.55) | copy-start | bytes 9437188
  294.8 5.7 %copy-start.2 = (bf16[1,384,4096]{2,1,0:T(8,128)(2,1)S(1)}, bf16[1,384,4096]{2,1,0:T(8,128)(2,1)}, u32[]{:S(2)}) copy-start(bf16[1,384,4096]{2,1,0:T(8,128)(2,1)} %mul.166) | copy-start | bytes 9437188
  304.2 2.7 copy-start
  307.1 3.5 collective-permute-start
  313.0 8.3 %copy-start.11 = (f32[16,8]{0,1:T(8,128)S(1)}, f32[16,8]{0,1:T(8,128)}, u32[]{:S(2)}) copy-start(f32[16,8]{0,1:T(8,128)} %param.29) | copy-start | bytes 1540
  315.7 61.0 %all-to-all-start.1 = ((bf16[128,3,2048]{2,1,0:T(4,128)(2,1)}), bf16[128,3,2048]{2,1,0:T(4,128)(2,1)S(1)}, u32[]{:S(2)}, u32[]{:S(2)}) async-start(bf16[128,3,2048]{2,1,0:T(4,128)(2,1)} %copy.57), calls=%async_computation.2 | async-start | bytes 4194304 | tf_op jit(solution)/shard_map/all_to_all | solution.py:167
  379.4 2.0 copy-start.7
  379.4 2.0 copy-start.8
Sparse Core Ops, SparseCore 0:
  9.8 109.6 all-gather.1
  123.6 33.4 reduce-scatter.1
where the time goes:
time: 390 us; the launch traced here: 389 us
  waiting for transfers between devices  187 us (48%)
  blocking collectives  76.7 us (20%)
  local copies, waits for them, and re-layouts  52.6 us (13%)
  starting transfers between devices  20.1 us (5%)
  matrix products  19.9 us (5%)
  other arithmetic  16.8 us (4%)
  between operations  15.7 us (4%)
    all_to_all x1, waiting for transfers between devices, shards(): lax.all_to_all(outgoing, ('ctx', 'exp'), split_axis=0, concat_axis=0, til...  78 us
    all_to_all x1, waiting for transfers between devices, shards(): lax.all_to_all((kept_cols + from_partner(given_cols.astype(jnp.bfloat16),...  55.4 us
    all_gather x1, blocking collectives, shards(): value_piece = lax.all_gather(value_head, 'ctx', axis=0, tiled=True)  42.7 us
    all_gather x1, blocking collectives, shards(): key_piece = lax.all_gather(key_head, 'ctx', axis=0, tiled=True)  34 us
    reduce_scatter x1, waiting for transfers between devices, shards(): lax.psum_scatter(partial_rows.astype(jnp.bfloat16), 'exp', scatter_dimens...  31.8 us
    all_gather x1, waiting for transfers between devices, shards(): lax.all_gather(out_weight, 'ctx', axis=1, tiled=True)  17.7 us
    unnamed x36, local copies, waits for them, and re-layouts  14.7 us
    all_to_all x1, starting transfers between devices, shards(): lax.all_to_all(outgoing, ('ctx', 'exp'), split_axis=0, concat_axis=0, til...  14.4 us
  transfers between devices with their start and end apart: 5, of which 5 were waited for; matrix products, arithmetic and copies ran while one was open for 9% of the time, Pallas kernels for 0%

commit v1 on v0

--- a/solution.py
+++ b/solution.py
@@ -3,6 +3,8 @@
 import jax
 import jax.numpy as jnp
 from jax import lax
+from jax.experimental import pallas as pl
+from jax.experimental.pallas import tpu as pltpu
 from jax.sharding import PartitionSpec as P
 
 QUERY_HEADS = 32
@@ -23,14 +25,417 @@
     return result_sum
 
 
-def dequant(values, exponents, lowest, highest):
-    row_blocks = exponents.shape[-2]
-    col_blocks = exponents.shape[-1]
-    row_rep = values.shape[-2] // row_blocks
-    col_rep = values.shape[-1] // col_blocks
-    factor = pow_two(exponents, lowest, highest).astype(jnp.bfloat16)
-    shaped = values.reshape(values.shape[:-2] + (row_blocks, row_rep, col_blocks, col_rep))
-    return (shaped * factor[..., :, None, :, None]).reshape(values.shape)
+MESH = pl.DeviceIdType.MESH
+F32 = jnp.float32
+BF16 = jnp.bfloat16
+NQ = 2
+
+
+def contract_first(lhs, rhs):
+    return lax.dot_general(lhs, rhs, (((0,), (0,)), ((), ())), preferred_element_type=F32)
+
+
+def remote(src, dst, send_sem, recv_sem, device):
+    return pltpu.make_async_remote_copy(
+        src_ref=src,
+        dst_ref=dst,
+        send_sem=send_sem,
+        recv_sem=recv_sem,
+        device_id=device,
+        device_id_type=MESH,
+    )
+
+
+class Place:
+    def __init__(self):
+        self.ctx = lax.axis_index("ctx")
+        self.exp = lax.axis_index("exp")
+        self.dp = lax.axis_index("dp")
+        self.z = self.ctx % 8
+        self.yh = self.ctx // 8
+        self.x = self.exp // 2
+        self.k = self.exp % 2
+        self.plane = self.yh * 4 + self.x
+
+    def at_z(self, dz, dk=0):
+        z = (self.z + dz) % 8
+        k = (self.k + dk) % 2
+        return {"ctx": self.yh * 8 + z, "exp": self.x * 2 + k, "dp": self.dp}
+
+    def at_plane(self, dx, dy):
+        x = (self.x + dx) % 4
+        yh = (self.yh + dy) % 2
+        dp = (self.dp + dy) % 2
+        return {"ctx": yh * 8 + self.z, "exp": x * 2 + self.k, "dp": dp}, yh * 4 + x
+
+    def plane_from(self, dx, dy):
+        return ((self.yh + 2 - dy) % 2) * 4 + (self.x + 4 - dx) % 4
+
+    def other_core(self):
+        return {"ctx": self.ctx, "exp": self.x * 2 + (1 - self.k), "dp": self.dp}
+
+
+PLANE = [(dx, dy) for dy in range(2) for dx in range(4)]
+
+
+def moe_kernel(
+    x_ref,
+    st_ref,
+    meta_ref,
+    gw_ref,
+    uw_ref,
+    dw_ref,
+    gs_ref,
+    us_ref,
+    ds_ref,
+    out_ref,
+    meta_in,
+    xg,
+    ys,
+    yr,
+    xo,
+    raw_g,
+    raw_u,
+    raw_d,
+    deq_g,
+    deq_u,
+    deq_d,
+    down_in,
+    hid,
+    hid_in,
+    os_,
+    orr,
+    comb,
+    sr,
+    rr,
+    sl,
+    rl,
+    fin,
+    fin_in,
+    w_sem,
+    meta_s,
+    meta_r,
+    zr_s,
+    zr_r,
+    zl_s,
+    zl_r,
+    pd_s,
+    pd_r,
+    fw_s,
+    fw_r,
+    one_s,
+    one_r,
+    ps_s,
+    ps_r,
+    br_s,
+    br_r,
+    bl_s,
+    bl_r,
+    fn_s,
+    fn_r,
+):
+    me = Place()
+    z, k = me.z, me.k
+    ch = xg.shape[-1]
+    partner = me.other_core()
+    right, left = me.at_z(1), me.at_z(7)
+    sends = []
+
+    loads = [
+        pltpu.make_async_copy(src, dst, w_sem.at[i])
+        for i, (src, dst) in enumerate(((gw_ref, raw_g), (uw_ref, raw_u), (dw_ref, raw_d)))
+    ]
+    for load in loads:
+        load.start()
+
+    barrier = pltpu.get_barrier_semaphore()
+    for i in range(1, 16):
+        pl.semaphore_signal(barrier, inc=1, device_id=me.at_z(i // 2, i % 2), device_id_type=MESH)
+    for dx, dy in PLANE[1:]:
+        pl.semaphore_signal(barrier, inc=1, device_id=me.at_plane(dx, dy)[0], device_id_type=MESH)
+    pl.semaphore_wait(barrier, 22)
+
+    def start(copy):
+        copy.start()
+        sends.append(copy)
+
+    for q in range(NQ):
+        xg[q, z] = x_ref[:, q * ch : (q + 1) * ch]
+
+    def ring(q, step, rightward):
+        block = (z + 8 - step) % 8 if rightward else (z + step) % 8
+        s_sem, r_sem = (zr_s, zr_r) if rightward else (zl_s, zl_r)
+        there = right if rightward else left
+        return remote(xg.at[q, block], xg.at[q, block], s_sem.at[q, step], r_sem.at[q, step], there)
+
+    def ring_wait(q, step, rightward):
+        block = (z + 7 - step) % 8 if rightward else (z + 1 + step) % 8
+        s_sem, r_sem = (zr_s, zr_r) if rightward else (zl_s, zl_r)
+        there = right if rightward else left
+        remote(
+            xg.at[q, block], xg.at[q, block], s_sem.at[q, step], r_sem.at[q, step], there
+        ).wait_recv()
+
+    for q in range(NQ):
+        start(ring(q, 0, True))
+        start(ring(q, 0, False))
+    for i in range(1, 16):
+        dz, dk = i // 2, i % 2
+        start(
+            remote(
+                meta_ref.at[(z + dz) % 8],
+                meta_in.at[i],
+                meta_s.at[i],
+                meta_r.at[i],
+                me.at_z(dz, dk),
+            )
+        )
+    meta_in[0] = meta_ref[z]
+
+    def scaled(raw, scale, deq):
+        def body(c, carry):
+            for half in range(2):
+                side = k if half == 0 else 1 - k
+                row = pl.multiple_of(c * 256 + side * 128, 128)
+                factor = scale[pl.ds(c * 2 + side, 1), :]
+                block = raw[pl.ds(row, 128), :].astype(F32) * factor
+                deq[half, pl.ds(pl.multiple_of(c * 128, 128), 128), :] = block.astype(BF16)
+            return carry
+
+        lax.fori_loop(0, 16, body, 0)
+
+    def scaled_down():
+        def body(c, carry):
+            for half in range(2):
+                side = k if half == 0 else 1 - k
+                col = pl.multiple_of(c * 256 + side * 128, 128)
+                to = pl.multiple_of(c * 128, 128)
+                for b in range(3):
+                    factor = ds_ref[b : b + 1, pl.ds(col, 128)]
+                    block = raw_d[b * 128 : (b + 1) * 128, pl.ds(col, 128)].astype(F32) * factor
+                    deq_d[half, b * 128 : (b + 1) * 128, pl.ds(to, 128)] = block.astype(BF16)
+            return carry
+
+        lax.fori_loop(0, 16, body, 0)
+
+    for step in range(1, 4):
+        loads[step - 1].wait()
+        if step == 1:
+            scaled(raw_g, gs_ref, deq_g)
+        elif step == 2:
+            scaled(raw_u, us_ref, deq_u)
+        else:
+            scaled_down()
+            start(remote(deq_d.at[1], down_in, one_s.at[0], one_r.at[0], partner))
+        for q in range(NQ):
+            ring_wait(q, step - 1, True)
+            start(ring(q, step, True))
+            if step < 3:
+                ring_wait(q, step - 1, False)
+                start(ring(q, step, False))
+
+    for i in range(1, 16):
+        remote(
+            meta_ref.at[z], meta_in.at[i], meta_s.at[i], meta_r.at[i], partner
+        ).wait_recv()
+    slots = meta_in[0]
+    for i in range(1, 16):
+        slots = slots + meta_in[i]
+    tokens = lax.broadcasted_iota(jnp.int32, (256, 384), 0).astype(F32) + 1.0
+    chosen = tokens == slots[0:1, :]
+    select = jnp.where(chosen, 1.0, 0.0).astype(BF16)
+    weights = jnp.where(chosen, slots[1:2, :], 0.0)
+    weights_hi = weights.astype(BF16)
+    weights_lo = (weights - weights_hi.astype(F32)).astype(BF16)
+
+    def to_plane(bufs, bufr, s_sem, r_sem, q, d):
+        device, there = me.at_plane(*PLANE[d])
+        return remote(
+            bufs.at[q, there], bufr.at[q, me.plane], s_sem.at[q, d], r_sem.at[q, d], device
+        )
+
+    def from_plane(bufr, s_sem, r_sem, q, d):
+        came = me.plane_from(*PLANE[d])
+        remote(
+            bufr.at[q, came], bufr.at[q, came], s_sem.at[q, d], r_sem.at[q, d], partner
+        ).wait_recv()
+        return came
+
+    for q in range(NQ):
+        ring_wait(q, 3, True)
+        ring_wait(q, 2, False)
+        picked = contract_first(select, xg[q].reshape(256, ch)).astype(BF16)
+        ys[q] = picked.reshape(8, 48, ch)
+        for d in range(1, 8):
+            start(to_plane(ys, yr, pd_s, pd_r, q, d))
+        yr[q, me.plane] = ys[q, me.plane]
+        start(
+            remote(
+                yr.at[q, me.plane], xo.at[q, me.plane], fw_s.at[q, 0], fw_r.at[q, 0], partner
+            )
+        )
+
+    gate = jnp.zeros((384, 384), F32)
+    up = jnp.zeros((384, 384), F32)
+    for q in range(NQ):
+        for d in range(1, 8):
+            came = from_plane(yr, pd_s, pd_r, q, d)
+            start(remote(yr.at[q, came], xo.at[q, came], fw_s.at[q, d], fw_r.at[q, d], partner))
+        for d in range(8):
+            came = me.plane_from(*PLANE[d])
+            remote(
+                yr.at[q, came], xo.at[q, came], fw_s.at[q, d], fw_r.at[q, d], partner
+            ).wait_recv()
+        for half, rows in ((0, yr), (1, xo)):
+            block = rows[q].reshape(384, ch)
+            gate = gate + jnp.dot(
+                block, deq_g[half, q * ch : (q + 1) * ch, :], preferred_element_type=F32
+            )
+            up = up + jnp.dot(
+                block, deq_u[half, q * ch : (q + 1) * ch, :], preferred_element_type=F32
+            )
+    hid[...] = (gate / (1.0 + jnp.exp(-gate)) * up).astype(BF16)
+    swap = remote(hid, hid_in, one_s.at[1], one_r.at[1], partner)
+    start(swap)
+    remote(deq_d.at[1], down_in, one_s.at[0], one_r.at[0], partner).wait_recv()
+    swap.wait_recv()
+
+    for q in range(NQ):
+        cols = slice(q * ch, (q + 1) * ch)
+        result = jnp.dot(hid[...], deq_d[0, :, cols], preferred_element_type=F32)
+        result = result + jnp.dot(hid_in[...], down_in[:, cols], preferred_element_type=F32)
+        os_[q] = result.astype(BF16).reshape(8, 48, ch)
+        for d in range(1, 8):
+            start(to_plane(os_, orr, ps_s, ps_r, q, d))
+        orr[q, me.plane] = os_[q, me.plane]
+
+    def back(q, step, rightward):
+        if rightward:
+            return remote(sr.at[q, step], rr.at[q, step], br_s.at[q, step], br_r.at[q, step], right)
+        return remote(sl.at[q, step], rl.at[q, step], bl_s.at[q, step], bl_r.at[q, step], left)
+
+    for q in range(NQ):
+        for d in range(1, 8):
+            from_plane(orr, ps_s, ps_r, q, d)
+        rows = orr[q].reshape(384, ch)
+        total = jnp.dot(weights_hi, rows, preferred_element_type=F32)
+        total = total + jnp.dot(weights_lo, rows, preferred_element_type=F32)
+        comb[q] = total.reshape(8, 32, ch)
+        sr[q, 0] = comb[q, (z + 4) % 8].astype(BF16)
+        start(back(q, 0, True))
+        sl[q, 0] = comb[q, (z + 5) % 8].astype(BF16)
+        start(back(q, 0, False))
+    for step in range(1, 4):
+        for q in range(NQ):
+            back(q, step - 1, True).wait_recv()
+            sr[q, step] = (rr[q, step - 1].astype(F32) + comb[q, (z + 4 - step) % 8]).astype(BF16)
+            start(back(q, step, True))
+            if step < 3:
+                back(q, step - 1, False).wait_recv()
+                sl[q, step] = (
+                    rl[q, step - 1].astype(F32) + comb[q, (z + 5 + step) % 8]
+                ).astype(BF16)
+                start(back(q, step, False))
+    for q in range(NQ):
+        back(q, 3, True).wait_recv()
+        back(q, 2, False).wait_recv()
+        total = comb[q, z] + rr[q, 3].astype(F32) + rl[q, 2].astype(F32)
+        total = total + st_ref[:, q * ch : (q + 1) * ch]
+        fin[q] = total.astype(BF16).reshape(2, 16, ch)
+        start(remote(fin.at[q, 1 - k], fin_in.at[q], fn_s.at[q], fn_r.at[q], partner))
+    for q in range(NQ):
+        remote(fin.at[q, 1 - k], fin_in.at[q], fn_s.at[q], fn_r.at[q], partner).wait_recv()
+        own, got = fin[q, k], fin_in[q]
+        for c in range(ch // 128):
+            at = (q * (ch // 128) + c) * 256
+            piece = slice(c * 128, (c + 1) * 128)
+            out_ref[:, pl.ds(pl.multiple_of(at + k * 128, 128), 128)] = own[:, piece]
+            out_ref[:, pl.ds(pl.multiple_of(at + (1 - k) * 128, 128), 128)] = got[:, piece]
+    for copy in sends:
+        copy.wait_send()
+
+
+def moe(x, state, meta, gate_w, up_w, down_w, gate_s, up_s, down_s):
+    width = x.shape[1]
+    ch = width // NQ
+    vmem = pl.BlockSpec(memory_space=pltpu.VMEM)
+    hbm = pl.BlockSpec(memory_space=pl.ANY)
+    dma = pltpu.SemaphoreType.DMA
+    return pl.pallas_call(
+        moe_kernel,
+        out_shape=jax.ShapeDtypeStruct((x.shape[0] // 2, 2 * width), BF16),
+        in_specs=[vmem, vmem, vmem, hbm, hbm, hbm, vmem, vmem, vmem],
+        out_specs=vmem,
+        scratch_shapes=[
+            pltpu.VMEM((16, 8, 384), F32),
+            pltpu.VMEM((NQ, 8, 32, ch), BF16),
+            pltpu.VMEM((NQ, 8, 48, ch), BF16),
+            pltpu.VMEM((NQ, 8, 48, ch), BF16),
+            pltpu.VMEM((NQ, 8, 48, ch), BF16),
+            pltpu.VMEM(gate_w.shape, BF16),
+            pltpu.VMEM(up_w.shape, BF16),
+            pltpu.VMEM(down_w.shape, BF16),
+            pltpu.VMEM((2, width, 384), BF16),
+            pltpu.VMEM((2, width, 384), BF16),
+            pltpu.VMEM((2, 384, width), BF16),
+            pltpu.VMEM((384, width), BF16),
+            pltpu.VMEM((384, 384), BF16),
+            pltpu.VMEM((384, 384), BF16),
+            pltpu.VMEM((NQ, 8, 48, ch), BF16),
+            pltpu.VMEM((NQ, 8, 48, ch), BF16),
+            pltpu.VMEM((NQ, 8, 32, ch), F32),
+            pltpu.VMEM((NQ, 4, 32, ch), BF16),
+            pltpu.VMEM((NQ, 4, 32, ch), BF16),
+            pltpu.VMEM((NQ, 3, 32, ch), BF16),
+            pltpu.VMEM((NQ, 3, 32, ch), BF16),
+            pltpu.VMEM((NQ, 2, 16, ch), BF16),
+            pltpu.VMEM((NQ, 16, ch), BF16),
+            dma((3,)),
+            dma((16,)),
+            dma((16,)),
+            dma((NQ, 4)),
+            dma((NQ, 4)),
+            dma((NQ, 3)),
+            dma((NQ, 3)),
+            dma((NQ, 8)),
+            dma((NQ, 8)),
+            dma((NQ, 8)),
+            dma((NQ, 8)),
+            dma((2,)),
+            dma((2,)),
+            dma((NQ, 8)),
+            dma((NQ, 8)),
+            dma((NQ, 4)),
+            dma((NQ, 4)),
+            dma((NQ, 3)),
+            dma((NQ, 3)),
+            dma((NQ,)),
+            dma((NQ,)),
+        ],
+        compiler_params=pltpu.CompilerParams(
+            collective_id=1, has_side_effects=True, vmem_limit_bytes=58 * 1024 * 1024
+        ),
+        name="experts",
+    )(x, state, meta, gate_w, up_w, down_w, gate_s, up_s, down_s)
+
+
+def routing(expert_ids, route_weight, my_ctx, my_exp):
+    z, k = my_ctx % 8, my_exp % 2
+    rows = expert_ids.shape[0]
+    named = expert_ids[:, :, None] == jnp.arange(64, dtype=jnp.int32)[None, None, :]
+    member = jnp.sum(named.astype(F32), axis=1)
+    weight = jnp.sum(jnp.where(named, route_weight[:, :, None], 0.0), axis=1)
+    earlier = jnp.arange(rows)[:, None] > jnp.arange(rows)[None, :]
+    slot = jnp.sum(jnp.where(earlier[:, :, None], member[None], 0.0), axis=1)
+    number = (z * 32 + k * 16 + 1 + jnp.arange(rows, dtype=jnp.int32)).astype(F32)
+    at = (slot[:, :, None] == jnp.arange(3).astype(F32)) & (member[:, :, None] > 0.5)
+    token = jnp.sum(jnp.where(at, number[:, None, None], 0.0), axis=0)
+    gain = jnp.sum(jnp.where(at, weight[:, :, None], 0.0), axis=0)
+    both = jnp.stack([token, gain], axis=0).reshape(2, 2, 8, 4, 3)
+    both = both.transpose(2, 0, 1, 3, 4).reshape(8, 2, 8, 1, 1, 3)
+    here = (jnp.arange(8) == z)[:, None, None] & (jnp.arange(2) == k)[None, :, None]
+    spread = jnp.where(here[None, None, None], both, 0.0).reshape(8, 2, 384)
+    return jnp.concatenate([spread, jnp.zeros((8, 6, 384), F32)], axis=1)
 
 
 def shards(
@@ -57,14 +462,11 @@
     query_group_width = QUERY_HEADS // KEY_VALUE_HEADS
     ctx_count = lax.axis_size("ctx")
     exp_count = lax.axis_size("exp")
-    experts = ctx_count * exp_count // 2
     tok_count = residual.shape[0]
     model_width = residual.shape[1]
     half_width = model_width // 2
-    capacity = min(tok_count, max(2, 3 * tok_count * TOP // (2 * experts)))
     my_ctx = lax.axis_index("ctx")
     my_exp = lax.axis_index("exp")
-    half_bit = my_exp % 2
     kv_head = my_exp * head_count // query_group_width
     ctx_ids = jnp.arange(ctx_count, dtype=jnp.int32)
 
@@ -139,49 +541,29 @@
     state_rows = residual.astype(jnp.float32) + mixed
     mean_sq = jnp.mean(state_rows * state_rows, axis=-1, keepdims=True)
     normed = (state_rows * lax.rsqrt(mean_sq + 1e-06) * norm_gain).astype(jnp.bfloat16)
-    flat_ids = expert_ids.reshape(-1)
-    onehot = (flat_ids[:, None] == jnp.arange(experts, dtype=jnp.int32)[None, :]).astype(jnp.int32)
-    before = jnp.cumsum(onehot, axis=0) - onehot
-    slot_ids = jnp.sum(before * onehot, axis=1)
-    target = flat_ids * capacity + slot_ids
-    owner_token = jnp.arange(flat_ids.shape[0], dtype=jnp.int32) // TOP
-    slot_table = jnp.full((experts * capacity,), tok_count, jnp.int32).at[target].set(owner_token)
-    padded = jnp.concatenate([normed, jnp.zeros((1, model_width), jnp.bfloat16)], axis=0)
-    outgoing = padded[slot_table].reshape(experts, 1, capacity, model_width)
-    outgoing = jnp.broadcast_to(outgoing, (experts, 2, capacity, model_width)).reshape(
-        2 * experts, capacity, model_width
+    k = my_exp % 2
+
+    def own_half(rows):
+        tiles = rows.reshape(tok_count, 16, 2, 128)
+        kept = lax.dynamic_index_in_dim(tiles, k, 2, False).reshape(tok_count, half_width)
+        given = lax.dynamic_index_in_dim(tiles, 1 - k, 2, False).reshape(tok_count, half_width)
+        came = from_partner(given, "exp", 0)
+        return jnp.where(k == 0, jnp.concatenate([kept, came]), jnp.concatenate([came, kept]))
+
+    def expanded(scale):
+        return jnp.repeat(pow_two(scale, -1, 1), 128, axis=1)
+
+    return moe(
+        own_half(normed),
+        own_half(state_rows),
+        routing(expert_ids, route_weight, my_ctx, my_exp),
+        gate_weight[0],
+        up_weight[0],
+        down_weight[0],
+        expanded(gate_scale[0]),
+        expanded(up_scale[0]),
+        expanded(down_scale[0]),
     )
-    gate_deq = dequant(gate_weight[0], gate_scale[0], -1, 1)
-    up_deq = dequant(up_weight[0], up_scale[0], -1, 1)
-    down_deq = dequant(down_weight[0], down_scale[0], -1, 1)
-    arrived = lax.all_to_all(outgoing, ("ctx", "exp"), split_axis=0, concat_axis=0, tiled=True)
-    flat_rows = arrived.reshape(-1, model_width)
-    gate_act = jnp.dot(flat_rows, gate_deq, preferred_element_type=jnp.float32)
-    up_act = jnp.dot(flat_rows, up_deq, preferred_element_type=jnp.float32)
-    hidden = (jax.nn.silu(gate_act) * up_act).astype(jnp.bfloat16)
-    partial_out = jnp.dot(hidden, down_deq, preferred_element_type=jnp.float32).reshape(
-        arrived.shape[0], arrived.shape[1], model_width
-    )
-    kept_cols = lax.dynamic_slice_in_dim(partial_out, half_bit * half_width, half_width, 2)
-    given_cols = lax.dynamic_slice_in_dim(partial_out, (1 - half_bit) * half_width, half_width, 2)
-    returned = lax.all_to_all(
-        (
-            kept_cols
-            + from_partner(given_cols.astype(jnp.bfloat16), "exp", 0).astype(given_cols.dtype)
-        ).astype(jnp.bfloat16),
-        ("ctx", "exp"),
-        split_axis=0,
-        concat_axis=0,
-        tiled=True,
-    )
-    expert_out = (
-        returned.reshape(experts, 2, capacity, half_width)
-        .transpose(0, 2, 1, 3)
-        .reshape(experts * capacity, model_width)
-    )
-    picked = expert_out[target].astype(jnp.float32) * route_weight.reshape(-1)[:, None]
-    combined = jnp.sum(picked.reshape(tok_count, TOP, model_width), axis=1)
-    return (state_rows + combined).astype(jnp.bfloat16)
 
 
 def solution(mesh):

time: 390 us -> 265 us (0.68)
  waiting for transfers between devices: 187 us -> 54.8 us
  Pallas kernels: 0 us -> 89.1 us
  local copies, waits for them, and re-layouts: 52.6 us -> 8.89 us
  starting transfers between devices: 20.1 us -> 3.5 us
  matrix products: 19.9 us -> 6.89 us
  other arithmetic: 16.8 us -> 12.1 us
    all_to_all x2 -> x0, waiting for transfers between devices: 133 us -> none  [the longest x1 78 us: shards(): lax.all_to_all(outgoing, ('ctx', 'exp'), split_axis=0, concat_axis=0, til...]
    pallas_call x0 -> x1, Pallas kernels: none -> 89.1 us  [moe(): pl.pallas_call(moe_kernel, out_shape=jax.ShapeDtypeStruct((x.shape[0] //...]
    all_to_all x2 -> x0, starting transfers between devices: 19.9 us -> none  [the longest x1 14.4 us: shards(): lax.all_to_all(outgoing, ('ctx', 'exp'), split_axis=0, concat_axis=0, til...]
    dot_general x3 -> x0, matrix products: 13 us -> none  [the longest x1 4.79 us: shards(): gate_act = jnp.dot(flat_rows, gate_deq, preferred_element_type=jnp.float32)]
    mul x8 -> x0, local copies, waits for them, and re-layouts: 11.7 us -> none  [the longest x6 11.6 us: dequant(): return (shaped * factor[..., :, None, :, None]).reshape(values.shape)]
    all_gather x1, blocking collectives: 42.7 us -> 32.3 us  [shards(): value_piece = lax.all_gather(value_head, 'ctx', axis=0, tiled=True)]
    unnamed x36 -> x22, local copies, waits for them, and re-layouts: 14.7 us -> 5.23 us
    reshape x2, local copies, waits for them, and re-layouts: 8.04 us -> 0.31 us  [own_half(): tiles = rows.reshape(tok_count, 16, 2, 128)]
  transfers between devices with their start and end apart: 5 -> 4, of which waited for: 5 -> 3; matrix products, arithmetic and copies ran while one was open for 9% -> 7% of each run, Pallas kernels for 0% -> 0%
where the time goes in v1:
time: 265 us; the launch traced here: 264 us
  Pallas kernels  89.1 us (34%)
  blocking collectives  73.4 us (28%)
  waiting for transfers between devices  54.8 us (21%)
  between operations  15.7 us (6%)
  other arithmetic  12.1 us (5%)
  local copies, waits for them, and re-layouts  8.89 us (3%)
  matrix products  6.89 us (3%)
  starting transfers between devices  3.5 us (1%)
    pallas_call x1, Pallas kernels, moe(): pl.pallas_call(moe_kernel, out_shape=jax.ShapeDtypeStruct((x.shape[0] //...  89.1 us
    all_gather x1, blocking collectives, shards(): key_piece = lax.all_gather(key_head, 'ctx', axis=0, tiled=True)  41.1 us
    all_gather x1, blocking collectives, shards(): value_piece = lax.all_gather(value_head, 'ctx', axis=0, tiled=True)  32.3 us
    reduce_scatter x1, waiting for transfers between devices, shards(): lax.psum_scatter(partial_rows.astype(jnp.bfloat16), 'exp', scatter_dimens...  29.5 us
    all_gather x1, waiting for transfers between devices, shards(): lax.all_gather(out_weight, 'ctx', axis=1, tiled=True)  23.9 us
  transfers between devices with their start and end apart: 4, of which 3 were waited for; matrix products, arithmetic and copies ran while one was open for 7% of the time, Pallas kernels for 0%

profile of v1, /device:TPU:1, one launch (start us, length us, event | category | flops | bytes accessed | tf_op | source)
XLA Modules:
  0.0 264.4 jit_solution(3805112550672653434)
XLA Ops:
  6.5 0.7 all-gather.2.cloned.1.call-update
  7.3 0.0 reduce-scatter.2.cloned.1.call-start
  7.3 1.3 fusion.39
  9.3 0.6 iota_add_fusion
  9.9 0.8 select_reduce_fusion.1
  10.7 0.6 fusion.41
  12.6 0.9 fusion.38
  13.5 0.1 broadcast_in_dim.245
  13.5 0.1 broadcast_in_dim.246
  13.6 0.9 fusion.37
  14.5 0.1 broadcast_in_dim.247
  14.6 0.1 broadcast_in_dim.248
  14.7 0.8 copy.62
  15.4 0.8 copy.63
  16.2 0.8 multiply_convert_fusion.2
  17.0 0.8 multiply_convert_fusion.1
  17.9 41.1 %all_gather.9 = bf16[2048,128]{1,0:T(8,128)(2,1)S(1)} all-gather(bf16[128,128]{1,0:T(8,128)(2,1)S(1)} %multiply_convert_fusion.2), channel_id=1, replica_groups=mesh['ctx'=16,'exp'=8,'dp'=2] {'ctx'}, dimensions={0}, use_global_device_ids=true | all-gather | bytes 557056 | tf_op jit(solution)/shard_map/all_gather | solution.py:496
  58.9 32.3 %all_gather.10 = bf16[2048,128]{1,0:T(8,128)(2,1)S(1)} all-gather(bf16[128,128]{1,0:T(8,128)(2,1)S(1)} %multiply_convert_fusion.1), channel_id=1, replica_groups=mesh['ctx'=16,'exp'=8,'dp'=2] {'ctx'}, dimensions={0}, use_global_device_ids=true | all-gather | bytes 557056 | tf_op jit(solution)/shard_map/all_gather | solution.py:497
  91.3 4.5 %conditional.1 = (f32[4,128]{1,0:T(4,128)S(1)}, f32[128,4,128]{0,2,1:T(8,128)S(1)}) conditional(s32[]{:T(128)} %convert_element_type.51, () %tuple.13, (s32[2048]{0:T(1024)S(1)}, s32[128]{0:T(128)S(1)}, bf16[128,512]{1,0:T(8,128)(2,1)}, bf16[2048,128]{1,0:T(8,128)(2,1)S(1)}, bf16[2048,128]{1,0:T(8,128)(2,1)S(1)}) %tuple.14), branch_computations={%region_4.5_spmd, %region_5.8_spmd} | conditional | flops 550764032 | bytes 15618576 | solution.py:527
  91.3 0.3 broadcast_compare_fusion
  91.6 1.6 fusion
  93.3 1.0 fusion.2
  94.3 1.3 fusion.6
  95.6 0.1 copy.73
  95.8 0.0 copy-start.3
  95.8 0.0 copy-start.4
  95.8 0.0 copy-start.2
  95.9 23.9 %all-gather.2.cloned.1.call-done = bf16[512,4096]{1,0:T(8,128)(2,1)} async-done(((bf16[512,256]{1,0:T(8,128)(2,1)}), bf16[512,4096]{1,0:T(8,128)(2,1)}) %all-gather.2.cloned.1.call-update) | async-done | bytes 4194320 | tf_op jit(solution)/shard_map/all_gather | solution.py:535
  119.8 3.9 %convolution_convert_fusion = bf16[128,4096]{1,0:T(8,128)(2,1)} fusion(bf16[128,512]{0,1:T(8,128)(2,1)S(1)} %bitcast.94, bf16[512,4096]{1,0:T(8,128)(2,1)} %all-gather.2.cloned.1.call-done), kind=kOutput, calls=%fused_computation.18 | convolution fusion | flops 537395200 | bytes 5373952 | tf_op jit(solution)/shard_map/dot_general | solution.py:533
  123.7 0.0 reduce-scatter.2.cloned.1.call-update
  123.8 0.1 convert_reduce_fusion
  123.9 0.1 select_reduce_fusion
  124.0 0.1 select_reduce_fusion.4
  124.1 0.1 stack.10
  124.2 0.1 stack.9
  124.3 0.1 copy.64
  124.5 0.1 broadcast_in_dim.261
  124.6 0.1 copy.66
  124.8 0.1 broadcast_and_fusion
  124.8 0.1 broadcast_in_dim.249
  124.9 0.2 broadcast_in_dim.250
  125.2 0.1 copy.70
  125.3 0.1 broadcast_in_dim.268
  125.4 0.6 copy.107
  126.0 0.1 copy.71
  126.1 0.1 broadcast_in_dim.269
  126.2 0.6 copy.106
  126.8 0.1 broadcast_bitcast_fusion
  126.9 0.7 copy.103
  127.6 0.6 concatenate.20.meta_ref
  128.2 29.5 %reduce-scatter.2.cloned.1.call-done = bf16[16,4096]{1,0:T(8,128)(2,1)} async-done(((bf16[128,4096]{1,0:T(8,128)(2,1)}), bf16[16,4096]{1,0:T(8,128)(2,1)}) %reduce-scatter.2.cloned.1.call-update) | async-done | bytes 131088 | tf_op jit(solution)/shard_map/reduce_scatter | solution.py:538
  157.8 1.1 convert_add_fusion
  158.8 1.0 multiply_convert_fusion
  159.9 0.1 reshape.255
  159.9 0.8 dynamic-slice_reduce_fusion.1
  160.7 3.2 %collective-permute-start = (bf16[16,2048]{1,0:T(8,128)(2,1)S(1)}, bf16[16,2048]{1,0:T(8,128)(2,1)S(1)}, u32[]{:S(2)}, u32[]{:S(2)}) collective-permute-start(bf16[16,2048]{1,0:T(8,128)(2,1)S(1)} %bitcast.107), channel_id=1, source_target_pairs={{0,2},{2,0},{4,6},{6,4},{8,10},{10,8},{12,14},{14,12},{1,3},{3,1},... | collective-permute-start | bytes 196616 | tf_op jit(solution)/shard_map/ppermute | solution.py:18
  163.9 0.2 reshape.258
  164.2 0.3 constant_dynamic-slice_fusion.1
  164.5 0.3 collective-permute-start.1
  164.8 0.7 maximum_select_fusion.1.x_ref
  165.5 0.6 collective-permute-done.1
  166.1 0.7 maximum_select_fusion.st_ref
  166.8 89.1 %experts.1 = bf16[16,4096]{1,0:T(8,128)(2,1)} custom-call(bf16[32,2048]{1,0:T(8,128)(2,1)} %maximum_select_fusion.1.x_ref, f32[32,2048]{1,0:T(8,128)} %maximum_select_fusion.st_ref, f32[8,8,384]{2,1,0:T(8,128)} %concatenate.20.meta_ref, bf16[4096,384]{1,0:T(8,128)(2,1)} %bitcast.87, bf16[4096,384]{1,0:T(8,128)(2,1)} %bitcast.88, bf16[384,4096]{1,0:T(8,128)(2,1)} %bitcast.89, ...), custom_call_target="tpu_custom_call" | custom-call | tf_op jit(solution)/shard_map/experts/pallas_call | solution.py:364
  256.0 1.6 copy.114
  (29 shorter events, 0.3 us)
Async XLA Ops:
  6.5 113.3 %all-gather.2.cloned.1.call-start = ((), (), s32[]{:S(2)}) async-start(), calls=%async_computation.1 | async-start | bytes 4456448 | tf_op jit(solution)/shard_map/all_gather | solution.py:535
  7.3 150.5 %reduce-scatter.2.cloned.1.call-start = ((), (), s32[]{:S(2)}) async-start(), calls=%async_computation.2 | async-start | bytes 1179648 | tf_op jit(solution)/shard_map/reduce_scatter | solution.py:538
  95.8 29.4 %copy-start.3 = (s32[1,32,3]{1,0,2:T(1,128)S(1)}, s32[1,32,3]{1,0,2:T(1,128)}, u32[]{:S(2)}) copy-start(s32[1,32,3]{1,0,2:T(1,128)} %param.31) | copy-start | bytes 1156
  95.8 29.4 %copy-start.4 = (s32[1,32,3]{1,0,2:T(1,128)S(1)}, s32[1,32,3]{1,0,2:T(1,128)}, u32[]{:S(2)}) copy-start(s32[1,32,3]{1,0,2:T(1,128)} %param.33) | copy-start | bytes 1156
  95.8 31.0 %copy-start.2 = (s32[1,3,32]{2,0,1:T(1,128)S(1)}, s32[1,3,32]{2,0,1:T(1,128)}, u32[]{:S(2)}) copy-start(s32[1,3,32]{2,0,1:T(1,128)} %param.35) | copy-start | bytes 1156
  119.8 38.0 %copy-start = (bf16[16,4096]{1,0:T(8,128)(2,1)S(1)}, bf16[16,4096]{1,0:T(8,128)(2,1)}, u32[]{:S(2)}) copy-start(bf16[16,4096]{1,0:T(8,128)(2,1)} %param.19) | copy-start | bytes 393220
  119.8 39.1 %copy-start.1 = (f32[4096]{0:T(1024)S(1)}, f32[4096]{0:T(1024)}, u32[]{:S(2)}) copy-start(f32[4096]{0:T(1024)} %param.27) | copy-start | bytes 49156
  160.7 4.1 %collective-permute-start = (bf16[16,2048]{1,0:T(8,128)(2,1)S(1)}, bf16[16,2048]{1,0:T(8,128)(2,1)S(1)}, u32[]{:S(2)}, u32[]{:S(2)}) collective-permute-start(bf16[16,2048]{1,0:T(8,128)(2,1)S(1)} %bitcast.107), channel_id=1, source_target_pairs={{0,2},{2,0},{4,6},{6,4},{8,10},{10,8},{12,14},{14,12},{1,3},{3,1},... | collective-permute-start | bytes 196616 | tf_op jit(solution)/shard_map/ppermute | solution.py:18
  164.5 1.6 collective-permute-start.1
Sparse Core Ops, SparseCore 0:
  9.8 109.9 all-gather.1
  123.9 33.8 reduce-scatter.1

commit v2 on v0

v2 whole, which is shorter than its diff:
```python
import math

import jax
import jax.numpy as jnp
from jax import lax
from jax.experimental import pallas as pl
from jax.experimental.pallas import tpu as pltpu
from jax.sharding import PartitionSpec as P

HEAD_SIZE = 128

MESH = pl.DeviceIdType.MESH
F32 = jnp.float32
BF16 = jnp.bfloat16
NQ = 2
OFFSETS = (0, 1, 7, 2, 6, 3, 5, 4)
GROUPS = ((0, 1), (1, 3), (3, 5), (5, 8))
PLANE = [(dx, dy) for dy in range(2) for dx in range(4)]


def contract_first(lhs, rhs):
    return lax.dot_general(lhs, rhs, (((0,), (0,)), ((), ())), preferred_element_type=F32)


def contract_last(lhs, rhs):
    return lax.dot_general(lhs, rhs, (((1,), (1,)), ((), ())), preferred_element_type=F32)


def mul(lhs, rhs):
    return jnp.dot(lhs, rhs, preferred_element_type=F32)


def remote(src, dst, send_sem, recv_sem, device):
    return pltpu.make_async_remote_copy(
        src_ref=src,
        dst_ref=dst,
        send_sem=send_sem,
        recv_sem=recv_sem,
        device_id=device,
        device_id_type=MESH,
    )


def hops(q):
    return (4, 3) if q % 2 == 0 else (3, 4)


class Place:
    def __init__(self):
        self.ctx = lax.axis_index("ctx")
        self.exp = lax.axis_index("exp")
        self.dp = lax.axis_index("dp")
        self.z = self.ctx % 8
        self.yh = self.ctx // 8
        self.x = self.exp // 2
        self.k = self.exp % 2
        self.plane = self.yh * 4 + self.x

    def at_ctx(self, i):
        return {"ctx": (self.ctx + i) % 16, "exp": self.exp, "dp": self.dp}

    def at_z(self, dz, dk=0):
        z = (self.z + dz) % 8
        k = (self.k + dk) % 2
        return {"ctx": self.yh * 8 + z, "exp": self.x * 2 + k, "dp": self.dp}

    def at_plane(self, dx, dy):
        x = (self.x + dx) % 4
        yh = (self.yh + dy) % 2
        dp = (self.dp + dy) % 2
        return {"ctx": yh * 8 + self.z, "exp": x * 2 + self.k, "dp": dp}, yh * 4 + x

    def plane_from(self, dx, dy):
        return ((self.yh + 2 - dy) % 2) * 4 + (self.x + 4 - dx) % 4

    def other_core(self):
        return {"ctx": self.ctx, "exp": self.x * 2 + (1 - self.k), "dp": self.dp}


def layer_kernel(
    q_ref,
    kq_ref,
    vq_ref,
    ke_ref,
    ve_ref,
    order_ref,
    w_ref,
    res_ref,
    gain_ref,
    meta_ref,
    gw_ref,
    uw_ref,
    dw_ref,
    gs_ref,
    us_ref,
    ds_ref,
    out_ref,
    *scratch_refs,
):
    r = dict(zip(SCRATCH, scratch_refs, strict=True))
    sem = {name[:-2]: (r[name], r[name[:-2] + "_r"]) for name in SCRATCH if name.endswith("_s")}
    me = Place()
    z, k, x, yh = me.z, me.k, me.x, me.yh
    partner = me.other_core()
    right, left = me.at_z(1), me.at_z(7)
    xg, st = r["xg"], r["st"]
    ch = xg.shape[-1]
    sends = []

    def start(copy):
        copy.start()
        sends.append(copy)

    def pair(name, *index):
        return sem[name][0].at[index], sem[name][1].at[index]

    loads = [
        pltpu.make_async_copy(src, r[dst], r["w_sem"].at[i])
        for i, (src, dst) in enumerate(((gw_ref, "raw_g"), (uw_ref, "raw_u"), (dw_ref, "raw_d")))
    ]
    for load in loads:
        load.start()

    barrier = pltpu.get_barrier_semaphore()
    peers = [me.at_ctx(i) for i in range(1, 16)] + [me.at_z(i, 1) for i in range(8)]
    peers = peers + [me.at_plane(dx, dy)[0] for dx, dy in PLANE[1:]]
    for peer in peers:
        pl.semaphore_signal(barrier, inc=1, device_id=peer, device_id_type=MESH)
    pl.semaphore_wait(barrier, len(peers))

    kv = r["kv"]
    row = lax.broadcasted_iota(jnp.int32, (128, 128), 0)
    col = lax.broadcasted_iota(jnp.int32, (128, 128), 1)
    head = pl.ds(pl.multiple_of(x * 128, 128), 128)
    first = jnp.where(k == 0, ke_ref[0, x], ve_ref[0, x])
    second = jnp.where(k == 0, ke_ref[1, x], ve_ref[1, x])
    power = jnp.where(row < 64, first, second)
    factor = jnp.zeros((128, 128), F32)
    for p in range(-2, 2):
        factor = factor + jnp.where(power == p, 2.0**p, 0.0)
    mine = jnp.where(k == 0, kq_ref[:, head].astype(F32), vq_ref[:, head].astype(F32))
    kv[k, me.ctx] = (mine * factor).astype(BF16)

    def kv_copy(i):
        return remote(kv.at[k, me.ctx], kv.at[k, me.ctx], *pair("kv", i), me.at_ctx(i))

    def kv_pass(i):
        src = (me.ctx + 16 - i) % 16
        return remote(kv.at[k, src], kv.at[k, src], *pair("kvp", i), partner)

    for i in range(1, 16):
        start(kv_copy(i))
    start(kv_pass(0))

    wb = r["wb"]
    wb[k, z] = w_ref[:, pl.ds(pl.multiple_of(k * 128, 128), 128)]
    give = w_ref.at[:, pl.ds(pl.multiple_of((1 - k) * 128, 128), 128)]

    def gather(buf, name, q, step, rightward):
        block = (z + 8 - step) % 8 if rightward else (z + step) % 8
        sems = pair(name + "r" if rightward else name + "l", q, step)
        return remote(buf(block), buf(block), *sems, right if rightward else left)

    def gathered(buf, name, q, step, rightward):
        block = (z + 7 - step) % 8 if rightward else (z + 1 + step) % 8
        sems = pair(name + "r" if rightward else name + "l", q, step)
        remote(buf(block), buf(block), *sems, right if rightward else left).wait_recv()

    def ring_start(buf, name, q):
        start(gather(buf, name, q, 0, True))
        start(gather(buf, name, q, 0, False))

    def ring_step(buf, name, q, step):
        rights, lefts = hops(q)
        for rightward, count in ((True, rights), (False, lefts)):
            if step < count:
                gathered(buf, name, q, step - 1, rightward)
                start(gather(buf, name, q, step, rightward))

    def ring_end(buf, name, q):
        rights, lefts = hops(q)
        gathered(buf, name, q, rights - 1, True)
        gathered(buf, name, q, lefts - 1, False)

    def w_block(q):
        core = k if q == 0 else 1 - k
        return lambda block: wb.at[core, block]

    start(remote(give, wb.at[k, z], *pair("one", 2), partner))
    ring_start(w_block(0), "w", 0)

    meta_in = r["meta_in"]
    for i in range(1, 16):
        dz, dk = i // 2, i % 2
        there = (z + dz) % 8
        start(remote(meta_ref.at[there], meta_in.at[i], *pair("meta", i), me.at_z(dz, dk)))
    meta_in[0] = meta_ref[z]

    res, res_give, gain = r["res"], r["res_give"], r["gain"]
    for c in range(16):
        to = slice(c * 128, (c + 1) * 128)
        own = pl.ds(pl.multiple_of(c * 256 + k * 128, 128), 128)
        other = pl.ds(pl.multiple_of(c * 256 + (1 - k) * 128, 128), 128)
        res[k, :, to] = res_ref[:, own]
        res_give[:, to] = res_ref[:, other]
        gain[:, to] = gain_ref[:, own]
    start(remote(res_give, res.at[k], *pair("one", 3), partner))

    def scaled(raw, scale, deq):
        def body(c, carry):
            for half in range(2):
                side = k if half == 0 else 1 - k
                at = pl.multiple_of(c * 256 + side * 128, 128)
                block = raw[pl.ds(at, 128), :].astype(F32) * scale[pl.ds(c * 2 + side, 1), :]
                deq[half, pl.ds(pl.multiple_of(c * 128, 128), 128), :] = block.astype(BF16)
            return carry

        lax.fori_loop(0, 16, body, 0)

    def scaled_down(raw, scale, deq):
        def body(c, carry):
            for half in range(2):
                side = k if half == 0 else 1 - k
                at = pl.ds(pl.multiple_of(c * 256 + side * 128, 128), 128)
                to = pl.ds(pl.multiple_of(c * 128, 128), 128)
                for b in range(3):
                    rows = slice(b * 128, (b + 1) * 128)
                    block = raw[rows, at].astype(F32) * scale[b : b + 1, at]
                    deq[half, rows, to] = block.astype(BF16)
            return carry

        lax.fori_loop(0, 16, body, 0)

    loads[0].wait()
    scaled(r["raw_g"], gs_ref, r["deq_g"])
    remote(give, wb.at[1 - k, z], *pair("one", 2), partner).wait_recv()
    ring_start(w_block(1), "w", 1)
    loads[1].wait()
    scaled(r["raw_u"], us_ref, r["deq_u"])
    loads[2].wait()
    scaled_down(r["raw_d"], ds_ref, r["deq_d"])
    start(remote(r["deq_d"].at[1], r["down_in"], *pair("one", 0), partner))

    bias = r["bias"]
    own_place = order_ref[me.ctx]
    for j in range(16):
        seen = order_ref[j] * 128 + col <= own_place * 128 + row
        bias[:, j * 128 : (j + 1) * 128] = jnp.where(seen, 0.0, -1e30)

    for i in range(1, 16):
        kv_copy(i).wait_recv()
        start(kv_pass(i))
        if i == 8:
            for q in range(2):
                ring_step(w_block(q), "w", q, 1)
    for i in range(16):
        src = (me.ctx + 16 - i) % 16
        remote(kv.at[1 - k, src], kv.at[1 - k, src], *pair("kvp", i), partner).wait_recv()

    ab = r["ab"]
    keys, values = kv[0].reshape(2048, 128), kv[1].reshape(2048, 128)
    for h in range(4):
        to = slice(h * 128, (h + 1) * 128)
        scores = contract_last(q_ref[:, to], keys) * (1.0 / math.sqrt(HEAD_SIZE) * math.log2(math.e))
        scores = scores + bias[...]
        exps = jnp.exp2(scores - jnp.max(scores, axis=1, keepdims=True))
        total = jnp.sum(exps, axis=1, keepdims=True)
        ab[k, yh, :, to] = (mul(exps.astype(BF16), values) / total).astype(BF16)
        if h % 2 == 0:
            for q in range(2):
                ring_step(w_block(q), "w", q, 2 + h // 2)
    start(remote(ab.at[k, yh], ab.at[k, yh], *pair("a", 0), partner))
    over = me.at_plane(0, 1)[0]
    start(remote(ab.at[k, yh], ab.at[k, yh], *pair("a", 1), over))
    came = ab.at[k, 1 - yh]
    remote(came, came, *pair("a", 1), over).wait_recv()
    start(remote(came, came, *pair("a", 2), partner))
    for i, there in ((0, yh), (2, 1 - yh)):
        came = ab.at[1 - k, there]
        remote(came, came, *pair("a", i), partner).wait_recv()

    px, rx, tot, yo, yi = r["px"], r["rx"], r["tot"], r["yo"], r["yi"]
    attended = [ab[core].reshape(256, 512) for core in range(2)]

    def x_copy(g, dx):
        lo, hi = GROUPS[g]
        part = pl.ds(lo, hi - lo)
        return remote(
            px.at[(x + dx) % 4, part], rx.at[dx, part], *pair("x", g, dx), me.at_plane(dx, 0)[0]
        )

    def y_copy(g):
        lo, hi = GROUPS[g]
        part = pl.ds(lo, hi - lo)
        return remote(yo.at[part], yi.at[part], *pair("y", g), over)

    for g, (lo, hi) in enumerate(GROUPS):
        for q in range(2):
            if g == len(GROUPS) - 1:
                ring_end(w_block(q), "w", q)
        if 0 < g < len(GROUPS) - 1:
            pass
        for n in range(lo, hi):
            at = (z + OFFSETS[n]) % 8
            part = mul(attended[0], wb[0, at]) + mul(attended[1], wb[1, at])
            part = part.astype(BF16).reshape(2, 4, 32, 128)
            for to in range(4):
                px[to, n] = part[:, to]
        for dx in range(1, 4):
            start(x_copy(g, dx))

    def place_columns(n, side, values):
        at = pl.ds(pl.multiple_of((side * 8 + (z + OFFSETS[n]) % 8) * 128, 128), 128)
        st[:, at] = values

    for g, (lo, hi) in enumerate(GROUPS):
        for dx in range(1, 4):
            x_copy(g, dx).wait_recv()
        for n in range(lo, hi):
            total = px[x, n].astype(F32)
            for dx in range(1, 4):
                total = total + rx[dx, n].astype(F32)
            tot[n] = total
            yo[n] = tot[n, 1 - yh].astype(BF16)
            place_columns(n, yh, tot[n, yh])
        start(y_copy(g))
    remote(res_give, res.at[1 - k], *pair("one", 3), partner).wait_recv()
    for g, (lo, hi) in enumerate(GROUPS):
        y_copy(g).wait_recv()
        for n in range(lo, hi):
            place_columns(n, 1 - yh, yi[n].astype(F32))
    st[...] = st[...] + res[...].reshape(32, 2048).astype(F32)
    squares = jnp.sum(st[...] * st[...], axis=1, keepdims=True)
    r["sq"][0] = jnp.broadcast_to(squares, (32, 128))
    swap = remote(r["sq"].at[0], r["sq"].at[1], *pair("one", 4), partner)
    start(swap)
    swap.wait_recv()
    mean = (r["sq"][0, :, 0:1] + r["sq"][1, :, 0:1]) / 4096.0
    normed = (st[...] * lax.rsqrt(mean + 1e-6) * gain[...]).astype(BF16)

    def x_block(q):
        return lambda block: xg.at[q, block]

    for q in range(NQ):
        xg[q, z] = normed[:, q * ch : (q + 1) * ch]
        ring_start(x_block(q), "z", q)

    for i in range(1, 16):
        remote(meta_ref.at[z], meta_in.at[i], *pair("meta", i), partner).wait_recv()
    slots = meta_in[0]
    for i in range(1, 16):
        slots = slots + meta_in[i]
    tokens = lax.broadcasted_iota(jnp.int32, (256, 384), 0).astype(F32) + 1.0
    chosen = tokens == slots[0:1, :]
    select = jnp.where(chosen, 1.0, 0.0).astype(BF16)
    weights = jnp.where(chosen, slots[1:2, :], 0.0)
    weights_hi = weights.astype(BF16)
    weights_lo = (weights - weights_hi.astype(F32)).astype(BF16)

    for step in range(1, 4):
        for q in range(NQ):
            ring_step(x_block(q), "z", q, step)

    def to_plane(bufs, bufr, name, q, d):
        device, there = me.at_plane(*PLANE[d])
        return remote(bufs.at[q, there], bufr.at[q, me.plane], *pair(name, q, d), device)

    def from_plane(bufr, name, q, d):
        came = me.plane_from(*PLANE[d])
        remote(bufr.at[q, came], bufr.at[q, came], *pair(name, q, d), partner).wait_recv()
        return came

    ys, yr, xo = r["ys"], r["yr"], r["xo"]
    for q in range(NQ):
        ring_end(x_block(q), "z", q)
        picked = contract_first(select, xg[q].reshape(256, ch)).astype(BF16)
        ys[q] = picked.reshape(8, 48, ch)
        for d in range(1, 8):
            start(to_plane(ys, yr, "pd", q, d))
        yr[q, me.plane] = ys[q, me.plane]
        start(remote(yr.at[q, me.plane], xo.at[q, me.plane], *pair("fw", q, 0), partner))

    gate = jnp.zeros((384, 384), F32)
    up = jnp.zeros((384, 384), F32)
    for q in range(NQ):
        for d in range(1, 8):
            came = from_plane(yr, "pd", q, d)
            start(remote(yr.at[q, came], xo.at[q, came], *pair("fw", q, d), partner))
        for d in range(8):
            came = me.plane_from(*PLANE[d])
            remote(yr.at[q, came], xo.at[q, came], *pair("fw", q, d), partner).wait_recv()
        for half, rows in ((0, yr), (1, xo)):
            block = rows[q].reshape(384, ch)
            gate = gate + mul(block, r["deq_g"][half, q * ch : (q + 1) * ch, :])
            up = up + mul(block, r["deq_u"][half, q * ch : (q + 1) * ch, :])
    hid, hid_in = r["hid"], r["hid_in"]
    hid[...] = (gate / (1.0 + jnp.exp(-gate)) * up).astype(BF16)
    swap = remote(hid, hid_in, *pair("one", 1), partner)
    start(swap)
    remote(r["deq_d"].at[1], r["down_in"], *pair("one", 0), partner).wait_recv()
    swap.wait_recv()

    es, er = r["es"], r["er"]
    for q in range(NQ):
        cols = slice(q * ch, (q + 1) * ch)
        result = mul(hid[...], r["deq_d"][0, :, cols]) + mul(hid_in[...], r["down_in"][:, cols])
        es[q] = result.astype(BF16).reshape(8, 48, ch)
        for d in range(1, 8):
            start(to_plane(es, er, "ps", q, d))
        er[q, me.plane] = es[q, me.plane]

    comb = r["comb"]

    def back(q, step, rightward):
        side, there = ("br", right) if rightward else ("bl", left)
        return remote(
            r[side + "_out"].at[q, step], r[side + "_in"].at[q, step], *pair(side, q, step), there
        )

    def back_start(q, step, rightward):
        rights, lefts = hops(q)
        side = "br" if rightward else "bl"
        block = (z + rights - step) % 8 if rightward else (z + 8 - lefts + step) % 8
        part = comb[q, block]
        if step:
            back(q, step - 1, rightward).wait_recv()
            part = part + r[side + "_in"][q, step - 1].astype(F32)
        r[side + "_out"][q, step] = part.astype(BF16)
        start(back(q, step, rightward))

    for q in range(NQ):
        for d in range(1, 8):
            from_plane(er, "ps", q, d)
        rows = er[q].reshape(384, ch)
        comb[q] = (mul(weights_hi, rows) + mul(weights_lo, rows)).reshape(8, 32, ch)
        back_start(q, 0, True)
        back_start(q, 0, False)
    for step in range(1, 4):
        for q in range(NQ):
            for rightward, count in zip((True, False), hops(q)):
                if step < count:
                    back_start(q, step, rightward)
    fin, fin_in = r["fin"], r["fin_in"]
    for q in range(NQ):
        total = comb[q, z] + st[:, q * ch : (q + 1) * ch]
        for rightward, count in zip((True, False), hops(q)):
            back(q, count - 1, rightward).wait_recv()
            total = total + r["br_in" if rightward else "bl_in"][q, count - 1].astype(F32)
        fin[q] = total.astype(BF16).reshape(2, 16, ch)
        start(remote(fin.at[q, 1 - k], fin_in.at[q], *pair("fn", q), partner))
    for q in range(NQ):
        remote(fin.at[q, 1 - k], fin_in.at[q], *pair("fn", q), partner).wait_recv()
        own, got = fin[q, k], fin_in[q]
        for c in range(ch // 128):
            at = (q * (ch // 128) + c) * 256
            piece = slice(c * 128, (c + 1) * 128)
            out_ref[:, pl.ds(pl.multiple_of(at + k * 128, 128), 128)] = own[:, piece]
            out_ref[:, pl.ds(pl.multiple_of(at + (1 - k) * 128, 128), 128)] = got[:, piece]
    for copy in sends:
        copy.wait_send()


def scratch():
    ch = 2048 // NQ
    shapes = {
        "kv": ((2, 16, 128, 128), BF16),
        "wb": ((2, 8, 512, 128), BF16),
        "res": ((2, 16, 2048), BF16),
        "res_give": ((16, 2048), BF16),
        "gain": ((1, 2048), F32),
        "bias": ((128, 2048), F32),
        "ab": ((2, 2, 128, 512), BF16),
        "px": ((4, 8, 2, 32, 128), BF16),
        "rx": ((4, 8, 2, 32, 128), BF16),
        "tot": ((8, 2, 32, 128), F32),
        "yo": ((8, 32, 128), BF16),
        "yi": ((8, 32, 128), BF16),
        "st": ((32, 2048), F32),
        "sq": ((2, 32, 128), F32),
        "meta_in": ((16, 8, 384), F32),
        "xg": ((NQ, 8, 32, ch), BF16),
        "ys": ((NQ, 8, 48, ch), BF16),
        "yr": ((NQ, 8, 48, ch), BF16),
        "xo": ((NQ, 8, 48, ch), BF16),
        "raw_g": ((4096, 384), BF16),
        "raw_u": ((4096, 384), BF16),
        "raw_d": ((384, 4096), BF16),
        "deq_g": ((2, 2048, 384), BF16),
        "deq_u": ((2, 2048, 384), BF16),
        "deq_d": ((2, 384, 2048), BF16),
        "down_in": ((384, 2048), BF16),
        "hid": ((384, 384), BF16),
        "hid_in": ((384, 384), BF16),
        "es": ((NQ, 8, 48, ch), BF16),
        "er": ((NQ, 8, 48, ch), BF16),
        "comb": ((NQ, 8, 32, ch), F32),
        "br_out": ((NQ, 4, 32, ch), BF16),
        "br_in": ((NQ, 4, 32, ch), BF16),
        "bl_out": ((NQ, 4, 32, ch), BF16),
        "bl_in": ((NQ, 4, 32, ch), BF16),
        "fin": ((NQ, 2, 16, ch), BF16),
        "fin_in": ((NQ, 16, ch), BF16),
    }
    made = {name: pltpu.VMEM(*what) for name, what in shapes.items()}
    made["w_sem"] = pltpu.SemaphoreType.DMA((3,))
    copies = {
        "kv": (16,),
        "kvp": (16,),
        "one": (5,),
        "wr": (2, 4),
        "wl": (2, 4),
        "meta": (16,),
        "a": (3,),
        "x": (len(GROUPS), 4),
        "y": (len(GROUPS),),
        "zr": (NQ, 4),
        "zl": (NQ, 4),
        "pd": (NQ, 8),
        "fw": (NQ, 8),
        "ps": (NQ, 8),
        "br": (NQ, 4),
        "bl": (NQ, 4),
        "fn": (NQ,),
    }
    for name, shape in copies.items():
        made[name + "_s"] = pltpu.SemaphoreType.DMA(shape)
        made[name + "_r"] = pltpu.SemaphoreType.DMA(shape)
    return made


SCRATCH = tuple(scratch())


def layer(*operands):
    vmem = pl.BlockSpec(memory_space=pltpu.VMEM)
    smem = pl.BlockSpec(memory_space=pltpu.SMEM)
    hbm = pl.BlockSpec(memory_space=pl.ANY)
    return pl.pallas_call(
        layer_kernel,
        out_shape=jax.ShapeDtypeStruct((16, 4096), BF16),
        in_specs=[vmem] * 3 + [smem] * 3 + [vmem] * 4 + [hbm] * 3 + [vmem] * 3,
        out_specs=vmem,
        scratch_shapes=list(scratch().values()),
        compiler_params=pltpu.CompilerParams(
            collective_id=1, has_side_effects=True, vmem_limit_bytes=58 * 1024 * 1024
        ),
        name="layer",
    )(*operands)


def pow_two(exponent, lowest, highest):
    result_sum = jnp.zeros(exponent.shape, jnp.float32)
    for power_of in range(lowest, highest + 1):
        result_sum = result_sum + jnp.where(exponent == power_of, 2.0**power_of, 0.0)
    return result_sum


def routing(expert_ids, route_weight, my_ctx, my_exp):
    z, k = my_ctx % 8, my_exp % 2
    rows = expert_ids.shape[0]
    named = expert_ids[:, :, None] == jnp.arange(64, dtype=jnp.int32)[None, None, :]
    member = jnp.sum(named.astype(F32), axis=1)
    weight = jnp.sum(jnp.where(named, route_weight[:, :, None], 0.0), axis=1)
    earlier = jnp.arange(rows)[:, None] > jnp.arange(rows)[None, :]
    slot = jnp.sum(jnp.where(earlier[:, :, None], member[None], 0.0), axis=1)
    number = (z * 32 + k * 16 + 1 + jnp.arange(rows, dtype=jnp.int32)).astype(F32)
    at = (slot[:, :, None] == jnp.arange(3).astype(F32)) & (member[:, :, None] > 0.5)
    token = jnp.sum(jnp.where(at, number[:, None, None], 0.0), axis=0)
    gain = jnp.sum(jnp.where(at, weight[:, :, None], 0.0), axis=0)
    both = jnp.stack([token, gain], axis=0).reshape(2, 2, 8, 4, 3)
    both = both.transpose(2, 0, 1, 3, 4).reshape(8, 2, 8, 1, 1, 3)
    here = (jnp.arange(8) == z)[:, None, None] & (jnp.arange(2) == k)[None, :, None]
    spread = jnp.where(here[None, None, None], both, 0.0).reshape(8, 2, 384)
    return jnp.concatenate([spread, jnp.zeros((8, 6, 384), F32)], axis=1)


def shards(
    residual,
    encoded_query_rows,
    quantized_key_rows,
    quantized_value_rows,
    key_block_exponent,
    value_block_exponent,
    block_order,
    out_weight,
    norm_gain,
    expert_ids,
    route_weight,
    gate_weight,
    gate_scale,
    up_weight,
    up_scale,
    down_weight,
    down_scale,
):
    def expanded(scale):
        return jnp.repeat(pow_two(scale, -1, 1), 128, axis=1)

    return layer(
        encoded_query_rows,
        quantized_key_rows,
        quantized_value_rows,
        key_block_exponent,
        value_block_exponent,
        block_order,
        out_weight,
        residual,
        norm_gain.reshape(1, -1),
        routing(expert_ids, route_weight, lax.axis_index("ctx"), lax.axis_index("exp")),
        gate_weight[0],
        up_weight[0],
        down_weight[0],
        expanded(gate_scale[0]),
        expanded(up_scale[0]),
        expanded(down_scale[0]),
    )


def solution(mesh):
    return jax.shard_map(
        shards,
        mesh=mesh,
        in_specs=(
            P(("dp", "ctx", "exp"), None),
            P(("dp", "ctx"), "exp"),
            P(("dp", "ctx"), None),
            P(("dp", "ctx"), None),
            P(("dp", "ctx"), None),
            P(("dp", "ctx"), None),
            P(),
            P("exp", "ctx"),
            P(),
            P(("dp", "ctx", "exp"), None),
            P(("dp", "ctx", "exp"), None),
            P(("ctx", "exp"), None, None),
            P(("ctx", "exp"), None, None),
            P(("ctx", "exp"), None, None),
            P(("ctx", "exp"), None, None),
            P(("ctx", "exp"), None, None),
            P(("ctx", "exp"), None, None),
        ),
        out_specs=P(("dp", "ctx", "exp"), None),
        check_vma=False,
    )
```

time: 390 us -> 156 us (0.40)
  waiting for transfers between devices: 187 us -> 0 us
  Pallas kernels: 0 us -> 147 us
  blocking collectives: 76.7 us -> 0 us
  local copies, waits for them, and re-layouts: 52.6 us -> 6.35 us
  starting transfers between devices: 20.1 us -> 0 us
  matrix products: 19.9 us -> 0 us
  between operations: 15.7 us -> 0.13 us
  other arithmetic: 16.8 us -> 2.52 us
    pallas_call x0 -> x1, Pallas kernels: none -> 147 us  [layer(): pl.pallas_call(layer_kernel, out_shape=jax.ShapeDtypeStruct((16, 4096), B...]
    all_to_all x2 -> x0, waiting for transfers between devices: 133 us -> none  [the longest x1 78 us: shards(): lax.all_to_all(outgoing, ('ctx', 'exp'), split_axis=0, concat_axis=0, til...]
    all_gather x2 -> x0, blocking collectives: 76.7 us -> none  [the longest x1 42.7 us: shards(): value_piece = lax.all_gather(value_head, 'ctx', axis=0, tiled=True)]
    reduce_scatter x1 -> x0, waiting for transfers between devices: 31.8 us -> none  [shards(): lax.psum_scatter(partial_rows.astype(jnp.bfloat16), 'exp', scatter_dimens...]
    all_to_all x2 -> x0, starting transfers between devices: 19.9 us -> none  [the longest x1 14.4 us: shards(): lax.all_to_all(outgoing, ('ctx', 'exp'), split_axis=0, concat_axis=0, til...]
    dot_general x6 -> x0, matrix products: 19.9 us -> none  [the longest x1 4.79 us: shards(): gate_act = jnp.dot(flat_rows, gate_deq, preferred_element_type=jnp.float32)]
    all_gather x1 -> x0, waiting for transfers between devices: 17.7 us -> none  [shards(): lax.all_gather(out_weight, 'ctx', axis=1, tiled=True)]
    mul x8 -> x0, local copies, waits for them, and re-layouts: 11.7 us -> none  [the longest x6 11.6 us: dequant(): return (shaped * factor[..., :, None, :, None]).reshape(values.shape)]
  transfers between devices with their start and end apart: 5 -> 0, of which waited for: 5 -> 0; matrix products, arithmetic and copies ran while one was open for 9% -> 0% of each run, Pallas kernels for 0% -> 0%
where the time goes in v2:
time: 156 us
  Pallas kernels  147 us (94%)
  local copies, waits for them, and re-layouts  6.35 us (4%)
  other arithmetic  2.52 us (2%)
    pallas_call x1, Pallas kernels, layer(): pl.pallas_call(layer_kernel, out_shape=jax.ShapeDtypeStruct((16, 4096), B...  147 us
    unnamed x6, local copies, waits for them, and re-layouts  3.82 us

profile of v2, /device:TPU:1, one launch (start us, length us, event | category | flops | bytes accessed | tf_op | source)
XLA Modules:
  0.0 156.1 jit_solution(12526799077706507809)
XLA Ops:
  0.0 0.8 copy.34
  0.8 0.8 copy.35
  1.5 0.1 convert_reduce_fusion
  1.7 0.1 select_reduce_fusion
  1.8 0.1 select_reduce_fusion.3
  1.9 0.1 stack.10
  2.0 0.1 stack.9
  2.1 0.1 copy.36
  2.3 0.1 broadcast_in_dim.157
  2.4 0.1 copy.38
  2.5 0.1 broadcast_and_fusion
  2.6 0.1 broadcast_in_dim.145
  2.7 0.2 broadcast_in_dim.146
  2.9 0.7 concatenate.4.meta_ref
  3.6 0.7 fusion.1
  4.3 0.1 copy.41
  4.4 0.1 broadcast_in_dim.164
  4.5 0.7 fusion.3
  5.2 0.1 copy.42
  5.3 0.1 broadcast_in_dim.165
  5.3 0.6 copy_bitcast_fusion.1
  6.0 0.7 fusion.5
  6.7 0.1 broadcast_bitcast_fusion
  6.8 0.7 copy.51
  7.4 147.1 %layer.1 = bf16[16,4096]{1,0:T(8,128)(2,1)} custom-call(bf16[128,512]{1,0:T(8,128)(2,1)} %q_ref.1, bf16[128,512]{1,0:T(8,128)(2,1)} %kq_ref.1, bf16[128,512]{1,0:T(8,128)(2,1)} %vq_ref.1, s32[2,4]{1,0:T(2,128)} %ke_ref.1, s32[2,4]{1,0:T(2,128)} %ve_ref.1, s32[16]{0:T(128)} %order_ref.1, bf16[512,256]{1,0:T(8,128)(2,1)} %w_ref.1, bf16[16,4096]{1,0:T(8,128)(2,1)} %res_ref.1, ...), custom_call_target="tpu_custom_call" | custom-call | tf_op jit(solution)/shard_map/layer/pallas_call | solution.py:538
  154.5 1.6 %copy.54 = bf16[16,4096]{1,0:T(8,128)(2,1)} copy(bf16[16,4096]{1,0:T(8,128)(2,1)} %layer.1) | data formatting | bytes 262144
  (10 shorter events, 0.1 us)

commit v3 on v2

--- a/solution.py
+++ b/solution.py
@@ -12,7 +12,7 @@
 MESH = pl.DeviceIdType.MESH
 F32 = jnp.float32
 BF16 = jnp.bfloat16
-NQ = 2
+NQ = 4
 OFFSETS = (0, 1, 7, 2, 6, 3, 5, 4)
 GROUPS = ((0, 1), (1, 3), (3, 5), (5, 8))
 PLANE = [(dx, dy) for dy in range(2) for dx in range(4)]
@@ -87,7 +87,8 @@
     w_ref,
     res_ref,
     gain_ref,
-    meta_ref,
+    ids_ref,
+    rw_ref,
     gw_ref,
     uw_ref,
     dw_ref,
@@ -122,11 +123,34 @@
         load.start()
 
     barrier = pltpu.get_barrier_semaphore()
-    peers = [me.at_ctx(i) for i in range(1, 16)] + [me.at_z(i, 1) for i in range(8)]
-    peers = peers + [me.at_plane(dx, dy)[0] for dx, dy in PLANE[1:]]
+    peers = [me.at_plane(dx, dy)[0] for dx, dy in PLANE[1:]]
+    peers = peers + [partner, right, left, me.at_ctx(8)]
     for peer in peers:
         pl.semaphore_signal(barrier, inc=1, device_id=peer, device_id_type=MESH)
     pl.semaphore_wait(barrier, len(peers))
+
+    def gather(buf, name, q, step, rightward):
+        block = (z + 8 - step) % 8 if rightward else (z + step) % 8
+        sems = pair(name + "r" if rightward else name + "l", q, step)
+        return remote(buf(block), buf(block), *sems, right if rightward else left)
+
+    def gathered(buf, name, q, step, rightward):
+        block = (z + 7 - step) % 8 if rightward else (z + 1 + step) % 8
+        sems = pair(name + "r" if rightward else name + "l", q, step)
+        remote(buf(block), buf(block), *sems, right if rightward else left).wait_recv()
+
+    def ring_start(buf, name, q):
+        start(gather(buf, name, q, 0, True))
+        start(gather(buf, name, q, 0, False))
+
+    def ring_step(buf, name, q, step, arrived=None):
+        for rightward, count in zip((True, False), hops(q)):
+            if step <= count:
+                gathered(buf, name, q, step - 1, rightward)
+                if step < count:
+                    start(gather(buf, name, q, step, rightward))
+                if arrived is not None:
+                    arrived(q, (8 - step if rightward else step) % 8)
 
     kv = r["kv"]
     row = lax.broadcasted_iota(jnp.int32, (128, 128), 0)
@@ -141,60 +165,50 @@
     mine = jnp.where(k == 0, kq_ref[:, head].astype(F32), vq_ref[:, head].astype(F32))
     kv[k, me.ctx] = (mine * factor).astype(BF16)
 
-    def kv_copy(i):
-        return remote(kv.at[k, me.ctx], kv.at[k, me.ctx], *pair("kv", i), me.at_ctx(i))
-
-    def kv_pass(i):
-        src = (me.ctx + 16 - i) % 16
-        return remote(kv.at[k, src], kv.at[k, src], *pair("kvp", i), partner)
-
-    for i in range(1, 16):
-        start(kv_copy(i))
-    start(kv_pass(0))
+    def kv_block(q):
+        side = yh if q == 0 else 1 - yh
+        return lambda block: kv.at[k, side * 8 + block]
+
+    def kv_pass(q, offset, kind=k):
+        at = kv.at[kind, (yh if q == 0 else 1 - yh) * 8 + (z + offset) % 8]
+        return remote(at, at, *pair("kvp", q, offset), partner)
+
+    def kv_arrived(q, offset):
+        start(kv_pass(q, offset))
+
+    own_kv = kv.at[k, me.ctx]
+    start(remote(own_kv, own_kv, *pair("one", 5), me.at_ctx(8)))
+    ring_start(kv_block(0), "kv", 0)
+    kv_arrived(0, 0)
+
+    mt = r["mt"]
+    mt[z, k] = jnp.zeros((2, 16, 128), F32)
+    mt[z, k, 0, :, 0:8] = ids_ref[...].astype(F32)
+    mt[z, k, 1, :, 0:8] = rw_ref[...]
+
+    def mt_block(block):
+        return mt.at[block, k]
+
+    def mt_pass(offset, core=k):
+        at = mt.at[(z + offset) % 8, core]
+        return remote(at, at, *pair("mtp", offset), partner)
+
+    def mt_arrived(q, offset):
+        start(mt_pass(offset))
+
+    ring_start(mt_block, "mt", 0)
+    mt_arrived(0, 0)
 
     wb = r["wb"]
     wb[k, z] = w_ref[:, pl.ds(pl.multiple_of(k * 128, 128), 128)]
     give = w_ref.at[:, pl.ds(pl.multiple_of((1 - k) * 128, 128), 128)]
 
-    def gather(buf, name, q, step, rightward):
-        block = (z + 8 - step) % 8 if rightward else (z + step) % 8
-        sems = pair(name + "r" if rightward else name + "l", q, step)
-        return remote(buf(block), buf(block), *sems, right if rightward else left)
-
-    def gathered(buf, name, q, step, rightward):
-        block = (z + 7 - step) % 8 if rightward else (z + 1 + step) % 8
-        sems = pair(name + "r" if rightward else name + "l", q, step)
-        remote(buf(block), buf(block), *sems, right if rightward else left).wait_recv()
-
-    def ring_start(buf, name, q):
-        start(gather(buf, name, q, 0, True))
-        start(gather(buf, name, q, 0, False))
-
-    def ring_step(buf, name, q, step):
-        rights, lefts = hops(q)
-        for rightward, count in ((True, rights), (False, lefts)):
-            if step < count:
-                gathered(buf, name, q, step - 1, rightward)
-                start(gather(buf, name, q, step, rightward))
-
-    def ring_end(buf, name, q):
-        rights, lefts = hops(q)
-        gathered(buf, name, q, rights - 1, True)
-        gathered(buf, name, q, lefts - 1, False)
-
     def w_block(q):
         core = k if q == 0 else 1 - k
         return lambda block: wb.at[core, block]
 
     start(remote(give, wb.at[k, z], *pair("one", 2), partner))
     ring_start(w_block(0), "w", 0)
-
-    meta_in = r["meta_in"]
-    for i in range(1, 16):
-        dz, dk = i // 2, i % 2
-        there = (z + dz) % 8
-        start(remote(meta_ref.at[there], meta_in.at[i], *pair("meta", i), me.at_z(dz, dk)))
-    meta_in[0] = meta_ref[z]
 
     res, res_give, gain = r["res"], r["res_give"], r["gain"]
     for c in range(16):
@@ -206,13 +220,19 @@
         gain[:, to] = gain_ref[:, own]
     start(remote(res_give, res.at[k], *pair("one", 3), partner))
 
+    def power_of(exponent):
+        return jnp.where(exponent == 0, 1.0, jnp.where(exponent > 0, 2.0, 0.5))
+
     def scaled(raw, scale, deq):
         def body(c, carry):
             for half in range(2):
                 side = k if half == 0 else 1 - k
-                at = pl.multiple_of(c * 256 + side * 128, 128)
-                block = raw[pl.ds(at, 128), :].astype(F32) * scale[pl.ds(c * 2 + side, 1), :]
-                deq[half, pl.ds(pl.multiple_of(c * 128, 128), 128), :] = block.astype(BF16)
+                at = pl.ds(pl.multiple_of(c * 256 + side * 128, 128), 128)
+                to = pl.ds(pl.multiple_of(c * 128, 128), 128)
+                for b in range(3):
+                    cols = slice(b * 128, (b + 1) * 128)
+                    block = raw[at, cols].astype(F32) * power_of(scale[c * 2 + side, b])
+                    deq[half, to, cols] = block.astype(BF16)
             return carry
 
         lax.fori_loop(0, 16, body, 0)
@@ -225,21 +245,18 @@
                 to = pl.ds(pl.multiple_of(c * 128, 128), 128)
                 for b in range(3):
                     rows = slice(b * 128, (b + 1) * 128)
-                    block = raw[rows, at].astype(F32) * scale[b : b + 1, at]
+                    block = raw[rows, at].astype(F32) * power_of(scale[b, c * 2 + side])
                     deq[half, rows, to] = block.astype(BF16)
             return carry
 
         lax.fori_loop(0, 16, body, 0)
 
-    loads[0].wait()
-    scaled(r["raw_g"], gs_ref, r["deq_g"])
+    across = kv.at[k, (1 - yh) * 8 + z]
+    remote(across, across, *pair("one", 5), me.at_ctx(8)).wait_recv()
+    ring_start(kv_block(1), "kv", 1)
+    kv_arrived(1, 0)
     remote(give, wb.at[1 - k, z], *pair("one", 2), partner).wait_recv()
     ring_start(w_block(1), "w", 1)
-    loads[1].wait()
-    scaled(r["raw_u"], us_ref, r["deq_u"])
-    loads[2].wait()
-    scaled_down(r["raw_d"], ds_ref, r["deq_d"])
-    start(remote(r["deq_d"].at[1], r["down_in"], *pair("one", 0), partner))
 
     bias = r["bias"]
     own_place = order_ref[me.ctx]
@@ -247,15 +264,18 @@
         seen = order_ref[j] * 128 + col <= own_place * 128 + row
         bias[:, j * 128 : (j + 1) * 128] = jnp.where(seen, 0.0, -1e30)
 
-    for i in range(1, 16):
-        kv_copy(i).wait_recv()
-        start(kv_pass(i))
-        if i == 8:
-            for q in range(2):
-                ring_step(w_block(q), "w", q, 1)
-    for i in range(16):
-        src = (me.ctx + 16 - i) % 16
-        remote(kv.at[1 - k, src], kv.at[1 - k, src], *pair("kvp", i), partner).wait_recv()
+    for step in range(1, 5):
+        for q in range(2):
+            ring_step(kv_block(q), "kv", q, step, kv_arrived)
+        ring_step(mt_block, "mt", 0, step, mt_arrived)
+        if step == 1:
+            loads[0].wait()
+            scaled(r["raw_g"], gs_ref, r["deq_g"])
+        if step >= 3:
+            ring_step(w_block(step - 3), "w", step - 3, 1)
+    for q in range(2):
+        for offset in range(8):
+            kv_pass(q, offset, 1 - k).wait_recv()
 
     ab = r["ab"]
     keys, values = kv[0].reshape(2048, 128), kv[1].reshape(2048, 128)
@@ -266,12 +286,36 @@
         exps = jnp.exp2(scores - jnp.max(scores, axis=1, keepdims=True))
         total = jnp.sum(exps, axis=1, keepdims=True)
         ab[k, yh, :, to] = (mul(exps.astype(BF16), values) / total).astype(BF16)
-        if h % 2 == 0:
-            for q in range(2):
-                ring_step(w_block(q), "w", q, 2 + h // 2)
+        ring_step(w_block(h % 2), "w", h % 2, 2 + h // 2)
+    over = me.at_plane(0, 1)[0]
     start(remote(ab.at[k, yh], ab.at[k, yh], *pair("a", 0), partner))
-    over = me.at_plane(0, 1)[0]
     start(remote(ab.at[k, yh], ab.at[k, yh], *pair("a", 1), over))
+
+    for offset in range(8):
+        mt_pass(offset, 1 - k).wait_recv()
+    table = mt[...].reshape(16, 2, 16, 128)
+    ids, rw = table[:, 0].reshape(256, 128), table[:, 1].reshape(256, 128)
+    slot = lax.broadcasted_iota(jnp.int32, (256, 384), 1)
+    token = lax.broadcasted_iota(jnp.int32, (256, 384), 0)
+    expert = slot // 48
+    named = ((expert // 4) * 32 + z * 4 + expert % 4).astype(F32)
+    member = jnp.zeros((256, 384), F32)
+    weights = jnp.zeros((256, 384), F32)
+    for n in range(8):
+        hit = ids[:, n : n + 1] == named
+        member = jnp.where(hit, 1.0, member)
+        weights = jnp.where(hit, rw[:, n : n + 1], weights)
+    first = lax.broadcasted_iota(jnp.int32, (256, 256), 0)
+    second = lax.broadcasted_iota(jnp.int32, (256, 256), 1)
+    earlier = (second < first) & (second // 16 == first // 16)
+    number = mul(jnp.where(earlier, 1.0, 0.0).astype(BF16), member.astype(BF16))
+    here = (number == (slot % 3).astype(F32)) & ((slot % 48) // 3 == token // 16)
+    weights = jnp.where(here, weights, 0.0)
+    select, weights_hi, weights_lo = r["sel"], r["whi"], r["wlo"]
+    select[...] = jnp.where(here, member, 0.0).astype(BF16)
+    weights_hi[...] = weights.astype(BF16)
+    weights_lo[...] = (weights - weights.astype(BF16).astype(F32)).astype(BF16)
+
     came = ab.at[k, 1 - yh]
     remote(came, came, *pair("a", 1), over).wait_recv()
     start(remote(came, came, *pair("a", 2), partner))
@@ -295,11 +339,11 @@
         return remote(yo.at[part], yi.at[part], *pair("y", g), over)
 
     for g, (lo, hi) in enumerate(GROUPS):
-        for q in range(2):
-            if g == len(GROUPS) - 1:
-                ring_end(w_block(q), "w", q)
-        if 0 < g < len(GROUPS) - 1:
-            pass
+        if g == len(GROUPS) - 1:
+            loads[1].wait()
+            scaled(r["raw_u"], us_ref, r["deq_u"])
+            for q in range(2):
+                ring_step(w_block(q), "w", q, 4)
         for n in range(lo, hi):
             at = (z + OFFSETS[n]) % 8
             part = mul(attended[0], wb[0, at]) + mul(attended[1], wb[1, at])
@@ -308,6 +352,10 @@
                 px[to, n] = part[:, to]
         for dx in range(1, 4):
             start(x_copy(g, dx))
+
+    loads[2].wait()
+    scaled_down(r["raw_d"], ds_ref, r["deq_d"])
+    start(remote(r["deq_d"].at[1], r["down_in"], *pair("one", 0), partner))
 
     def place_columns(n, side, values):
         at = pl.ds(pl.multiple_of((side * 8 + (z + OFFSETS[n]) % 8) * 128, 128), 128)
@@ -345,18 +393,6 @@
         xg[q, z] = normed[:, q * ch : (q + 1) * ch]
         ring_start(x_block(q), "z", q)
 
-    for i in range(1, 16):
-        remote(meta_ref.at[z], meta_in.at[i], *pair("meta", i), partner).wait_recv()
-    slots = meta_in[0]
-    for i in range(1, 16):
-        slots = slots + meta_in[i]
-    tokens = lax.broadcasted_iota(jnp.int32, (256, 384), 0).astype(F32) + 1.0
-    chosen = tokens == slots[0:1, :]
-    select = jnp.where(chosen, 1.0, 0.0).astype(BF16)
-    weights = jnp.where(chosen, slots[1:2, :], 0.0)
-    weights_hi = weights.astype(BF16)
-    weights_lo = (weights - weights_hi.astype(F32)).astype(BF16)
-
     for step in range(1, 4):
         for q in range(NQ):
             ring_step(x_block(q), "z", q, step)
@@ -372,8 +408,8 @@
 
     ys, yr, xo = r["ys"], r["yr"], r["xo"]
     for q in range(NQ):
-        ring_end(x_block(q), "z", q)
-        picked = contract_first(select, xg[q].reshape(256, ch)).astype(BF16)
+        ring_step(x_block(q), "z", q, 4)
+        picked = contract_first(select[...], xg[q].reshape(256, ch)).astype(BF16)
         ys[q] = picked.reshape(8, 48, ch)
         for d in range(1, 8):
             start(to_plane(ys, yr, "pd", q, d))
@@ -432,7 +468,7 @@
         for d in range(1, 8):
             from_plane(er, "ps", q, d)
         rows = er[q].reshape(384, ch)
-        comb[q] = (mul(weights_hi, rows) + mul(weights_lo, rows)).reshape(8, 32, ch)
+        comb[q] = (mul(weights_hi[...], rows) + mul(weights_lo[...], rows)).reshape(8, 32, ch)
         back_start(q, 0, True)
         back_start(q, 0, False)
     for step in range(1, 4):
@@ -477,7 +513,10 @@
         "yi": ((8, 32, 128), BF16),
         "st": ((32, 2048), F32),
         "sq": ((2, 32, 128), F32),
-        "meta_in": ((16, 8, 384), F32),
+        "mt": ((8, 2, 2, 16, 128), F32),
+        "sel": ((256, 384), BF16),
+        "whi": ((256, 384), BF16),
+        "wlo": ((256, 384), BF16),
         "xg": ((NQ, 8, 32, ch), BF16),
         "ys": ((NQ, 8, 48, ch), BF16),
         "yr": ((NQ, 8, 48, ch), BF16),
@@ -504,12 +543,15 @@
     made = {name: pltpu.VMEM(*what) for name, what in shapes.items()}
     made["w_sem"] = pltpu.SemaphoreType.DMA((3,))
     copies = {
-        "kv": (16,),
-        "kvp": (16,),
-        "one": (5,),
+        "kvr": (2, 4),
+        "kvl": (2, 4),
+        "kvp": (2, 8),
+        "mtr": (1, 4),
+        "mtl": (1, 4),
+        "mtp": (8,),
+        "one": (6,),
         "wr": (2, 4),
         "wl": (2, 4),
-        "meta": (16,),
         "a": (3,),
         "x": (len(GROUPS), 4),
         "y": (len(GROUPS),),
@@ -538,7 +580,7 @@
     return pl.pallas_call(
         layer_kernel,
         out_shape=jax.ShapeDtypeStruct((16, 4096), BF16),
-        in_specs=[vmem] * 3 + [smem] * 3 + [vmem] * 4 + [hbm] * 3 + [vmem] * 3,
+        in_specs=[vmem] * 3 + [smem] * 3 + [vmem] * 5 + [hbm] * 3 + [smem] * 3,
         out_specs=vmem,
         scratch_shapes=list(scratch().values()),
         compiler_params=pltpu.CompilerParams(
@@ -546,32 +588,6 @@
         ),
         name="layer",
     )(*operands)
-
-
-def pow_two(exponent, lowest, highest):
-    result_sum = jnp.zeros(exponent.shape, jnp.float32)
-    for power_of in range(lowest, highest + 1):
-        result_sum = result_sum + jnp.where(exponent == power_of, 2.0**power_of, 0.0)
-    return result_sum
-
-
-def routing(expert_ids, route_weight, my_ctx, my_exp):
-    z, k = my_ctx % 8, my_exp % 2
-    rows = expert_ids.shape[0]
-    named = expert_ids[:, :, None] == jnp.arange(64, dtype=jnp.int32)[None, None, :]
-    member = jnp.sum(named.astype(F32), axis=1)
-    weight = jnp.sum(jnp.where(named, route_weight[:, :, None], 0.0), axis=1)
-    earlier = jnp.arange(rows)[:, None] > jnp.arange(rows)[None, :]
-    slot = jnp.sum(jnp.where(earlier[:, :, None], member[None], 0.0), axis=1)
-    number = (z * 32 + k * 16 + 1 + jnp.arange(rows, dtype=jnp.int32)).astype(F32)
-    at = (slot[:, :, None] == jnp.arange(3).astype(F32)) & (member[:, :, None] > 0.5)
-    token = jnp.sum(jnp.where(at, number[:, None, None], 0.0), axis=0)
-    gain = jnp.sum(jnp.where(at, weight[:, :, None], 0.0), axis=0)
-    both = jnp.stack([token, gain], axis=0).reshape(2, 2, 8, 4, 3)
-    both = both.transpose(2, 0, 1, 3, 4).reshape(8, 2, 8, 1, 1, 3)
-    here = (jnp.arange(8) == z)[:, None, None] & (jnp.arange(2) == k)[None, :, None]
-    spread = jnp.where(here[None, None, None], both, 0.0).reshape(8, 2, 384)
-    return jnp.concatenate([spread, jnp.zeros((8, 6, 384), F32)], axis=1)
 
 
 def shards(
@@ -593,9 +609,6 @@
     down_weight,
     down_scale,
 ):
-    def expanded(scale):
-        return jnp.repeat(pow_two(scale, -1, 1), 128, axis=1)
-
     return layer(
         encoded_query_rows,
         quantized_key_rows,
@@ -606,13 +619,14 @@
         out_weight,
         residual,
         norm_gain.reshape(1, -1),
-        routing(expert_ids, route_weight, lax.axis_index("ctx"), lax.axis_index("exp")),
+        expert_ids,
+        route_weight,
         gate_weight[0],
         up_weight[0],
         down_weight[0],
-        expanded(gate_scale[0]),
-        expanded(up_scale[0]),
-        expanded(down_scale[0]),
+        gate_scale[0],
+        up_scale[0],
+        down_scale[0],
     )
 
 

time: 156 us -> 143 us (0.917)
  Pallas kernels: 147 us -> 135 us
  other arithmetic: 2.52 us -> 0 us
  local copies, waits for them, and re-layouts: 6.35 us -> 8.25 us
    pallas_call x1, Pallas kernels: 147 us -> 135 us  [layer(): pl.pallas_call(layer_kernel, out_shape=jax.ShapeDtypeStruct((16, 4096), B...]
    squeeze x0 -> x2, local copies, waits for them, and re-layouts: none -> 2.72 us  [the longest x1 1.36 us: shards(): gate_scale[0]]
    add x3 -> x0, other arithmetic: 2.07 us -> none  [pow_two(): result_sum + jnp.where(exponent == power_of, 2.0 ** power_of, 0.0)]
    unnamed x6 -> x4, local copies, waits for them, and re-layouts: 3.82 us -> 5.53 us
where the time goes in v3:
time: 143 us
  Pallas kernels  135 us (94%)
  local copies, waits for them, and re-layouts  8.25 us (6%)
    pallas_call x1, Pallas kernels, layer(): pl.pallas_call(layer_kernel, out_shape=jax.ShapeDtypeStruct((16, 4096), B...  135 us
    unnamed x4, local copies, waits for them, and re-layouts  5.53 us

profile of v3, /device:TPU:1, one launch (start us, length us, event | category | flops | bytes accessed | tf_op | source)
XLA Modules:
  0.0 143.2 jit_solution(2710645399255598336)
XLA Ops:
  0.0 1.3 copy.26
  1.3 1.4 copy.18.ids_ref
  2.6 1.4 copy.19.rw_ref
  4.0 1.4 copy.22
  5.3 1.4 copy.23
  6.7 134.9 %layer.1 = bf16[16,4096]{1,0:T(8,128)(2,1)} custom-call(bf16[128,512]{1,0:T(8,128)(2,1)} %q_ref.1, bf16[128,512]{1,0:T(8,128)(2,1)} %kq_ref.1, bf16[128,512]{1,0:T(8,128)(2,1)} %vq_ref.1, s32[2,4]{1,0:T(2,128)} %ke_ref.1, s32[2,4]{1,0:T(2,128)} %ve_ref.1, s32[16]{0:T(128)} %order_ref.1, bf16[512,256]{1,0:T(8,128)(2,1)} %w_ref.1, bf16[16,4096]{1,0:T(8,128)(2,1)} %res_ref.1, ...), custom_call_target="tpu_custom_call" | custom-call | tf_op jit(solution)/shard_map/layer/pallas_call | solution.py:580
  141.6 1.6 %copy.28 = bf16[16,4096]{1,0:T(8,128)(2,1)} copy(bf16[16,4096]{1,0:T(8,128)(2,1)} %layer.1) | data formatting | bytes 262144

commit v4 on v3

--- a/solution.py
+++ b/solution.py
@@ -124,7 +124,7 @@
 
     barrier = pltpu.get_barrier_semaphore()
     peers = [me.at_plane(dx, dy)[0] for dx, dy in PLANE[1:]]
-    peers = peers + [partner, right, left, me.at_ctx(8)]
+    peers = peers + [partner, me.at_ctx(8)] + [me.at_z(i) for i in range(1, 8)]
     for peer in peers:
         pl.semaphore_signal(barrier, inc=1, device_id=peer, device_id_type=MESH)
     pl.semaphore_wait(barrier, len(peers))
@@ -165,50 +165,58 @@
     mine = jnp.where(k == 0, kq_ref[:, head].astype(F32), vq_ref[:, head].astype(F32))
     kv[k, me.ctx] = (mine * factor).astype(BF16)
 
-    def kv_block(q):
-        side = yh if q == 0 else 1 - yh
-        return lambda block: kv.at[k, side * 8 + block]
-
-    def kv_pass(q, offset, kind=k):
-        at = kv.at[kind, (yh if q == 0 else 1 - yh) * 8 + (z + offset) % 8]
-        return remote(at, at, *pair("kvp", q, offset), partner)
-
-    def kv_arrived(q, offset):
-        start(kv_pass(q, offset))
-
-    own_kv = kv.at[k, me.ctx]
-    start(remote(own_kv, own_kv, *pair("one", 5), me.at_ctx(8)))
-    ring_start(kv_block(0), "kv", 0)
-    kv_arrived(0, 0)
+    def kv_at(offset, side, kind=k):
+        return kv.at[kind, (yh if side == 0 else 1 - yh) * 8 + (z + offset) % 8]
+
+    def kv_copy(offset):
+        own = kv_at(0, 0)
+        return remote(own, own, *pair("kv", offset), me.at_z(offset))
+
+    def kv_across(offset):
+        at = kv_at(offset, 0)
+        return remote(at, at, *pair("kva", offset), me.at_ctx(8))
+
+    def kv_pass(offset, side):
+        at = kv_at(offset, side)
+        return remote(at, at, *pair("kvp", side, offset), partner)
+
+    for offset in (4, 3, 5, 2, 6, 1, 7):
+        start(kv_copy(offset))
+    start(kv_across(0))
+    start(kv_pass(0, 0))
 
     mt = r["mt"]
-    mt[z, k] = jnp.zeros((2, 16, 128), F32)
-    mt[z, k, 0, :, 0:8] = ids_ref[...].astype(F32)
-    mt[z, k, 1, :, 0:8] = rw_ref[...]
-
-    def mt_block(block):
-        return mt.at[block, k]
+    mt[z, k] = jnp.zeros((2, 8, 128), F32)
+    mt[z, k, 0, :, 0:16] = ids_ref[...].astype(F32)
+    mt[z, k, 1, :, 0:16] = rw_ref[...]
+
+    def mt_copy(offset):
+        return remote(mt.at[z, k], mt.at[z, k], *pair("mt", offset), me.at_z(offset))
 
     def mt_pass(offset, core=k):
         at = mt.at[(z + offset) % 8, core]
         return remote(at, at, *pair("mtp", offset), partner)
 
-    def mt_arrived(q, offset):
-        start(mt_pass(offset))
-
-    ring_start(mt_block, "mt", 0)
-    mt_arrived(0, 0)
+    for offset in range(1, 8):
+        start(mt_copy(offset))
+    start(mt_pass(0))
 
     wb = r["wb"]
     wb[k, z] = w_ref[:, pl.ds(pl.multiple_of(k * 128, 128), 128)]
     give = w_ref.at[:, pl.ds(pl.multiple_of((1 - k) * 128, 128), 128)]
 
     def w_block(q):
-        core = k if q == 0 else 1 - k
-        return lambda block: wb.at[core, block]
+        core = k if q < 2 else 1 - k
+        rows = pl.ds((q % 2) * 256, 256)
+        return lambda block: wb.at[core, block, rows]
+
+    def w_step(step, parts=range(4)):
+        for q in parts:
+            ring_step(w_block(q), "w", q, step)
 
     start(remote(give, wb.at[k, z], *pair("one", 2), partner))
-    ring_start(w_block(0), "w", 0)
+    for q in range(2):
+        ring_start(w_block(q), "w", q)
 
     res, res_give, gain = r["res"], r["res_give"], r["gain"]
     for c in range(16):
@@ -223,7 +231,7 @@
     def power_of(exponent):
         return jnp.where(exponent == 0, 1.0, jnp.where(exponent > 0, 2.0, 0.5))
 
-    def scaled(raw, scale, deq):
+    def scaled(raw, scale, deq, lo=0, hi=16):
         def body(c, carry):
             for half in range(2):
                 side = k if half == 0 else 1 - k
@@ -231,13 +239,13 @@
                 to = pl.ds(pl.multiple_of(c * 128, 128), 128)
                 for b in range(3):
                     cols = slice(b * 128, (b + 1) * 128)
-                    block = raw[at, cols].astype(F32) * power_of(scale[c * 2 + side, b])
+                    block = raw[at, cols].astype(F32) * power_of(scale[b, 0, c * 2 + side])
                     deq[half, to, cols] = block.astype(BF16)
             return carry
 
-        lax.fori_loop(0, 16, body, 0)
-
-    def scaled_down(raw, scale, deq):
+        lax.fori_loop(lo, hi, body, 0)
+
+    def scaled_down(raw, scale, deq, lo=0, hi=16):
         def body(c, carry):
             for half in range(2):
                 side = k if half == 0 else 1 - k
@@ -245,18 +253,15 @@
                 to = pl.ds(pl.multiple_of(c * 128, 128), 128)
                 for b in range(3):
                     rows = slice(b * 128, (b + 1) * 128)
-                    block = raw[rows, at].astype(F32) * power_of(scale[b, c * 2 + side])
+                    block = raw[rows, at].astype(F32) * power_of(scale[b, 0, c * 2 + side])
                     deq[half, rows, to] = block.astype(BF16)
             return carry
 
-        lax.fori_loop(0, 16, body, 0)
-
-    across = kv.at[k, (1 - yh) * 8 + z]
-    remote(across, across, *pair("one", 5), me.at_ctx(8)).wait_recv()
-    ring_start(kv_block(1), "kv", 1)
-    kv_arrived(1, 0)
+        lax.fori_loop(lo, hi, body, 0)
+
     remote(give, wb.at[1 - k, z], *pair("one", 2), partner).wait_recv()
-    ring_start(w_block(1), "w", 1)
+    for q in range(2, 4):
+        ring_start(w_block(q), "w", q)
 
     bias = r["bias"]
     own_place = order_ref[me.ctx]
@@ -264,18 +269,26 @@
         seen = order_ref[j] * 128 + col <= own_place * 128 + row
         bias[:, j * 128 : (j + 1) * 128] = jnp.where(seen, 0.0, -1e30)
 
-    for step in range(1, 5):
-        for q in range(2):
-            ring_step(kv_block(q), "kv", q, step, kv_arrived)
-        ring_step(mt_block, "mt", 0, step, mt_arrived)
-        if step == 1:
-            loads[0].wait()
-            scaled(r["raw_g"], gs_ref, r["deq_g"])
-        if step >= 3:
-            ring_step(w_block(step - 3), "w", step - 3, 1)
-    for q in range(2):
+    loads[0].wait()
+    scaled(r["raw_g"], gs_ref, r["deq_g"])
+    for offset in (1, 7, 2, 6, 3, 5, 4):
+        came = kv_at(8 - offset, 0)
+        remote(came, came, *pair("kv", offset), partner).wait_recv()
+        start(kv_across(8 - offset))
+        start(kv_pass(8 - offset, 0))
+    w_step(1)
+    for offset in range(1, 8):
+        came = mt.at[(z + 8 - offset) % 8, k]
+        remote(came, came, *pair("mt", offset), partner).wait_recv()
+        start(mt_pass(8 - offset))
+    for offset in (0, 7, 1, 6, 2, 5, 3, 4):
+        came = kv_at(offset, 1)
+        remote(came, came, *pair("kva", offset), partner).wait_recv()
+        start(kv_pass(offset, 1))
+    for side in range(2):
         for offset in range(8):
-            kv_pass(q, offset, 1 - k).wait_recv()
+            came = kv_at(offset, side, 1 - k)
+            remote(came, came, *pair("kvp", side, offset), partner).wait_recv()
 
     ab = r["ab"]
     keys, values = kv[0].reshape(2048, 128), kv[1].reshape(2048, 128)
@@ -286,15 +299,21 @@
         exps = jnp.exp2(scores - jnp.max(scores, axis=1, keepdims=True))
         total = jnp.sum(exps, axis=1, keepdims=True)
         ab[k, yh, :, to] = (mul(exps.astype(BF16), values) / total).astype(BF16)
-        ring_step(w_block(h % 2), "w", h % 2, 2 + h // 2)
+        if h == 1:
+            w_step(2, range(2))
+    w_step(2, range(2, 4))
     over = me.at_plane(0, 1)[0]
     start(remote(ab.at[k, yh], ab.at[k, yh], *pair("a", 0), partner))
     start(remote(ab.at[k, yh], ab.at[k, yh], *pair("a", 1), over))
 
     for offset in range(8):
         mt_pass(offset, 1 - k).wait_recv()
-    table = mt[...].reshape(16, 2, 16, 128)
-    ids, rw = table[:, 0].reshape(256, 128), table[:, 1].reshape(256, 128)
+    tables = r["tables"]
+    for n in range(16):
+        for kind in range(2):
+            block = jnp.transpose(mt[n // 2, n % 2, kind])
+            tables[kind, n * 16 : (n + 1) * 16, 0:8] = block[0:16, :]
+    ids, rw = tables[0], tables[1]
     slot = lax.broadcasted_iota(jnp.int32, (256, 384), 1)
     token = lax.broadcasted_iota(jnp.int32, (256, 384), 0)
     expert = slot // 48
@@ -316,6 +335,7 @@
     weights_hi[...] = weights.astype(BF16)
     weights_lo[...] = (weights - weights.astype(BF16).astype(F32)).astype(BF16)
 
+    w_step(3)
     came = ab.at[k, 1 - yh]
     remote(came, came, *pair("a", 1), over).wait_recv()
     start(remote(came, came, *pair("a", 2), partner))
@@ -342,8 +362,7 @@
         if g == len(GROUPS) - 1:
             loads[1].wait()
             scaled(r["raw_u"], us_ref, r["deq_u"])
-            for q in range(2):
-                ring_step(w_block(q), "w", q, 4)
+            w_step(4)
         for n in range(lo, hi):
             at = (z + OFFSETS[n]) % 8
             part = mul(attended[0], wb[0, at]) + mul(attended[1], wb[1, at])
@@ -352,10 +371,6 @@
                 px[to, n] = part[:, to]
         for dx in range(1, 4):
             start(x_copy(g, dx))
-
-    loads[2].wait()
-    scaled_down(r["raw_d"], ds_ref, r["deq_d"])
-    start(remote(r["deq_d"].at[1], r["down_in"], *pair("one", 0), partner))
 
     def place_columns(n, side, values):
         at = pl.ds(pl.multiple_of((side * 8 + (z + OFFSETS[n]) % 8) * 128, 128), 128)
@@ -386,16 +401,27 @@
     mean = (r["sq"][0, :, 0:1] + r["sq"][1, :, 0:1]) / 4096.0
     normed = (st[...] * lax.rsqrt(mean + 1e-6) * gain[...]).astype(BF16)
 
-    def x_block(q):
-        return lambda block: xg.at[q, block]
-
     for q in range(NQ):
         xg[q, z] = normed[:, q * ch : (q + 1) * ch]
-        ring_start(x_block(q), "z", q)
-
-    for step in range(1, 4):
-        for q in range(NQ):
-            ring_step(x_block(q), "z", q, step)
+
+    def z_copy(q, source, to):
+        block = xg.at[q, (z + source) % 8]
+        return remote(block, block, *pair("z", q, (source - to) % 8), me.at_z(to % 8))
+
+    def z_wait(q, source):
+        block = xg.at[q, (z + source) % 8]
+        remote(block, block, *pair("z", q, source), partner).wait_recv()
+
+    def z_first(q):
+        for to in (2, -2, 1, -1):
+            start(z_copy(q, 0, to))
+
+    def z_second(q):
+        for side in (1, -1):
+            z_wait(q, (-2 * side) % 8)
+            start(z_copy(q, -2 * side, side))
+            if (side == 1) == (q % 2 == 0):
+                start(z_copy(q, -2 * side, 2 * side))
 
     def to_plane(bufs, bufr, name, q, d):
         device, there = me.at_plane(*PLANE[d])
@@ -407,14 +433,30 @@
         return came
 
     ys, yr, xo = r["ys"], r["yr"], r["xo"]
-    for q in range(NQ):
-        ring_step(x_block(q), "z", q, 4)
+    def pick(q):
         picked = contract_first(select[...], xg[q].reshape(256, ch)).astype(BF16)
         ys[q] = picked.reshape(8, 48, ch)
         for d in range(1, 8):
             start(to_plane(ys, yr, "pd", q, d))
         yr[q, me.plane] = ys[q, me.plane]
         start(remote(yr.at[q, me.plane], xo.at[q, me.plane], *pair("fw", q, 0), partner))
+
+    ahead = 2
+    for q in range(min(ahead, NQ)):
+        z_first(q)
+    loads[2].wait()
+    for turn in range(NQ + 1):
+        if turn < NQ:
+            if turn < 2:
+                scaled_down(r["raw_d"], ds_ref, r["deq_d"], turn * 8, turn * 8 + 8)
+            z_second(turn)
+            if turn + ahead < NQ:
+                z_first(turn + ahead)
+        if turn:
+            for source in (1, 7, 3, 5, 4):
+                z_wait(turn - 1, source)
+            pick(turn - 1)
+    start(remote(r["deq_d"].at[1], r["down_in"], *pair("one", 0), partner))
 
     gate = jnp.zeros((384, 384), F32)
     up = jnp.zeros((384, 384), F32)
@@ -447,41 +489,44 @@
 
     comb = r["comb"]
 
-    def back(q, step, rightward):
-        side, there = ("br", right) if rightward else ("bl", left)
+    towards = {1: 1, 7: -1, 3: 1, 5: -1, 2: 2, 6: -2}
+    back_out, back_in = r["back_out"], r["back_in"]
+
+    def back(q, offset):
+        to = towards.get(offset, 2 if q % 2 == 0 else -2)
         return remote(
-            r[side + "_out"].at[q, step], r[side + "_in"].at[q, step], *pair(side, q, step), there
+            back_out.at[q, offset], back_in.at[q, offset], *pair("b", q, offset), me.at_z(to % 8)
         )
 
-    def back_start(q, step, rightward):
-        rights, lefts = hops(q)
-        side = "br" if rightward else "bl"
-        block = (z + rights - step) % 8 if rightward else (z + 8 - lefts + step) % 8
-        part = comb[q, block]
-        if step:
-            back(q, step - 1, rightward).wait_recv()
-            part = part + r[side + "_in"][q, step - 1].astype(F32)
-        r[side + "_out"][q, step] = part.astype(BF16)
-        start(back(q, step, rightward))
-
-    for q in range(NQ):
-        for d in range(1, 8):
-            from_plane(er, "ps", q, d)
-        rows = er[q].reshape(384, ch)
-        comb[q] = (mul(weights_hi[...], rows) + mul(weights_lo[...], rows)).reshape(8, 32, ch)
-        back_start(q, 0, True)
-        back_start(q, 0, False)
-    for step in range(1, 4):
-        for q in range(NQ):
-            for rightward, count in zip((True, False), hops(q)):
-                if step < count:
-                    back_start(q, step, rightward)
+    def back_start(q, offset, came=()):
+        part = comb[q, (z + offset) % 8]
+        for other in came:
+            back(q, other).wait_recv()
+            part = part + back_in[q, other].astype(F32)
+        back_out[q, offset] = part.astype(BF16)
+        start(back(q, offset))
+
+    def back_second(q):
+        back_start(q, 2, (3, 4) if q % 2 == 0 else (3,))
+        back_start(q, 6, (5,) if q % 2 == 0 else (5, 4))
+
     fin, fin_in = r["fin"], r["fin_in"]
+    for turn in range(NQ + 1):
+        if turn < NQ:
+            for d in range(1, 8):
+                from_plane(er, "ps", turn, d)
+            rows = er[turn].reshape(384, ch)
+            total = mul(weights_hi[...], rows) + mul(weights_lo[...], rows)
+            comb[turn] = total.reshape(8, 32, ch)
+            for offset in (4, 3, 5, 1, 7):
+                back_start(turn, offset)
+        if turn:
+            back_second(turn - 1)
     for q in range(NQ):
         total = comb[q, z] + st[:, q * ch : (q + 1) * ch]
-        for rightward, count in zip((True, False), hops(q)):
-            back(q, count - 1, rightward).wait_recv()
-            total = total + r["br_in" if rightward else "bl_in"][q, count - 1].astype(F32)
+        for offset in (1, 7, 2, 6):
+            back(q, offset).wait_recv()
+            total = total + back_in[q, offset].astype(F32)
         fin[q] = total.astype(BF16).reshape(2, 16, ch)
         start(remote(fin.at[q, 1 - k], fin_in.at[q], *pair("fn", q), partner))
     for q in range(NQ):
@@ -513,7 +558,8 @@
         "yi": ((8, 32, 128), BF16),
         "st": ((32, 2048), F32),
         "sq": ((2, 32, 128), F32),
-        "mt": ((8, 2, 2, 16, 128), F32),
+        "mt": ((8, 2, 2, 8, 128), F32),
+        "tables": ((2, 256, 128), F32),
         "sel": ((256, 384), BF16),
         "whi": ((256, 384), BF16),
         "wlo": ((256, 384), BF16),
@@ -533,35 +579,30 @@
         "es": ((NQ, 8, 48, ch), BF16),
         "er": ((NQ, 8, 48, ch), BF16),
         "comb": ((NQ, 8, 32, ch), F32),
-        "br_out": ((NQ, 4, 32, ch), BF16),
-        "br_in": ((NQ, 4, 32, ch), BF16),
-        "bl_out": ((NQ, 4, 32, ch), BF16),
-        "bl_in": ((NQ, 4, 32, ch), BF16),
+        "back_out": ((NQ, 8, 32, ch), BF16),
+        "back_in": ((NQ, 8, 32, ch), BF16),
         "fin": ((NQ, 2, 16, ch), BF16),
         "fin_in": ((NQ, 16, ch), BF16),
     }
     made = {name: pltpu.VMEM(*what) for name, what in shapes.items()}
     made["w_sem"] = pltpu.SemaphoreType.DMA((3,))
     copies = {
-        "kvr": (2, 4),
-        "kvl": (2, 4),
+        "kv": (8,),
+        "kva": (8,),
         "kvp": (2, 8),
-        "mtr": (1, 4),
-        "mtl": (1, 4),
+        "mt": (8,),
         "mtp": (8,),
         "one": (6,),
-        "wr": (2, 4),
-        "wl": (2, 4),
+        "wr": (4, 4),
+        "wl": (4, 4),
         "a": (3,),
         "x": (len(GROUPS), 4),
         "y": (len(GROUPS),),
-        "zr": (NQ, 4),
-        "zl": (NQ, 4),
+        "z": (NQ, 8),
         "pd": (NQ, 8),
         "fw": (NQ, 8),
         "ps": (NQ, 8),
-        "br": (NQ, 4),
-        "bl": (NQ, 4),
+        "b": (NQ, 8),
         "fn": (NQ,),
     }
     for name, shape in copies.items():
@@ -619,14 +660,14 @@
         out_weight,
         residual,
         norm_gain.reshape(1, -1),
-        expert_ids,
-        route_weight,
+        expert_ids.T,
+        route_weight.T,
         gate_weight[0],
         up_weight[0],
         down_weight[0],
-        gate_scale[0],
-        up_scale[0],
-        down_scale[0],
+        gate_scale.transpose(2, 0, 1),
+        up_scale.transpose(2, 0, 1),
+        down_scale.transpose(1, 0, 2),
     )
 
 

time: 143 us -> 124 us (0.87)
  Pallas kernels: 135 us -> 122 us
  local copies, waits for them, and re-layouts: 8.25 us -> 1.57 us
    pallas_call x1, Pallas kernels: 135 us -> 122 us  [layer(): pl.pallas_call(layer_kernel, out_shape=jax.ShapeDtypeStruct((16, 4096), B...]
    unnamed x4 -> x1, local copies, waits for them, and re-layouts: 5.53 us -> 1.57 us
    squeeze x2 -> x0, local copies, waits for them, and re-layouts: 2.72 us -> none  [the longest x1 1.36 us: shards(): gate_scale[0]]
where the time goes in v4:
time: 124 us
  Pallas kernels  122 us (98%)
  local copies, waits for them, and re-layouts  1.57 us (1%)
    pallas_call x1, Pallas kernels, layer(): pl.pallas_call(layer_kernel, out_shape=jax.ShapeDtypeStruct((16, 4096), B...  122 us

profile of v4, /device:TPU:1, one launch (start us, length us, event | category | flops | bytes accessed | tf_op | source)
XLA Modules:
  0.0 123.8 jit_solution(7338749598277858061)
XLA Ops:
  0.0 122.3 %layer.1 = bf16[16,4096]{1,0:T(8,128)(2,1)} custom-call(bf16[128,512]{1,0:T(8,128)(2,1)} %q_ref.1, bf16[128,512]{1,0:T(8,128)(2,1)} %kq_ref.1, bf16[128,512]{1,0:T(8,128)(2,1)} %vq_ref.1, s32[2,4]{1,0:T(2,128)} %ke_ref.1, s32[2,4]{1,0:T(2,128)} %ve_ref.1, s32[16]{0:T(128)} %order_ref.1, bf16[512,256]{1,0:T(8,128)(2,1)} %w_ref.1, bf16[16,4096]{1,0:T(8,128)(2,1)} %res_ref.1, ...), custom_call_target="tpu_custom_call" | custom-call | tf_op jit(solution)/shard_map/layer/pallas_call | solution.py:621
  122.3 1.6 %copy.19 = bf16[16,4096]{1,0:T(8,128)(2,1)} copy(bf16[16,4096]{1,0:T(8,128)(2,1)} %layer.1) | data formatting | bytes 262144

commit v5 on v4

--- a/solution.py
+++ b/solution.py
@@ -14,7 +14,7 @@
 BF16 = jnp.bfloat16
 NQ = 4
 OFFSETS = (0, 1, 7, 2, 6, 3, 5, 4)
-GROUPS = ((0, 1), (1, 3), (3, 5), (5, 8))
+GROUPS = ((0, 3), (3, 5), (5, 8))
 PLANE = [(dx, dy) for dy in range(2) for dx in range(4)]
 
 
@@ -115,6 +115,19 @@
     def pair(name, *index):
         return sem[name][0].at[index], sem[name][1].at[index]
 
+    shared = []
+
+    def post(copy, *sent):
+        copy.start()
+        if sent:
+            shared.append(sent)
+
+    def shares(name, send, recv):
+        return sem[name][0].at[send], sem[name][1].at[recv]
+
+    def arrived(buf, name, recv):
+        remote(buf, buf, *shares(name, 0, recv), partner).wait_recv()
+
     loads = [
         pltpu.make_async_copy(src, r[dst], r["w_sem"].at[i])
         for i, (src, dst) in enumerate(((gw_ref, "raw_g"), (uw_ref, "raw_u"), (dw_ref, "raw_d")))
@@ -131,26 +144,23 @@
 
     def gather(buf, name, q, step, rightward):
         block = (z + 8 - step) % 8 if rightward else (z + step) % 8
-        sems = pair(name + "r" if rightward else name + "l", q, step)
+        sems = shares(name, 0, q * 8 + step * 2 + (0 if rightward else 1))
         return remote(buf(block), buf(block), *sems, right if rightward else left)
 
     def gathered(buf, name, q, step, rightward):
         block = (z + 7 - step) % 8 if rightward else (z + 1 + step) % 8
-        sems = pair(name + "r" if rightward else name + "l", q, step)
-        remote(buf(block), buf(block), *sems, right if rightward else left).wait_recv()
+        arrived(buf(block), name, q * 8 + step * 2 + (0 if rightward else 1))
 
     def ring_start(buf, name, q):
-        start(gather(buf, name, q, 0, True))
-        start(gather(buf, name, q, 0, False))
-
-    def ring_step(buf, name, q, step, arrived=None):
+        post(gather(buf, name, q, 0, True))
+        post(gather(buf, name, q, 0, False))
+
+    def ring_step(buf, name, q, step):
         for rightward, count in zip((True, False), hops(q)):
             if step <= count:
                 gathered(buf, name, q, step - 1, rightward)
                 if step < count:
-                    start(gather(buf, name, q, step, rightward))
-                if arrived is not None:
-                    arrived(q, (8 - step if rightward else step) % 8)
+                    post(gather(buf, name, q, step, rightward))
 
     kv = r["kv"]
     row = lax.broadcasted_iota(jnp.int32, (128, 128), 0)
@@ -170,36 +180,35 @@
 
     def kv_copy(offset):
         own = kv_at(0, 0)
-        return remote(own, own, *pair("kv", offset), me.at_z(offset))
+        return remote(own, own, *shares("kv", 0, offset), me.at_z(offset))
 
     def kv_across(offset):
         at = kv_at(offset, 0)
-        return remote(at, at, *pair("kva", offset), me.at_ctx(8))
-
-    def kv_pass(offset, side):
-        at = kv_at(offset, side)
-        return remote(at, at, *pair("kvp", side, offset), partner)
+        return remote(at, at, *shares("kva", 0, 0), me.at_ctx(8))
+
+    def kv_side(side, kind):
+        return kv.at[kind, pl.ds(pl.multiple_of((yh if side == 0 else 1 - yh) * 8, 8), 8)]
+
+    def kv_pass(side):
+        return remote(kv_side(side, k), kv_side(side, k), *pair("kvp", side), partner)
 
     for offset in (4, 3, 5, 2, 6, 1, 7):
-        start(kv_copy(offset))
-    start(kv_across(0))
-    start(kv_pass(0, 0))
+        post(kv_copy(offset))
+    post(kv_across(0))
+    shared.append((kv.at[0, pl.ds(0, 7)], "kv", 0))
+    shared.append((kv.at[0, pl.ds(0, 8)], "kva", 0))
 
     mt = r["mt"]
     mt[z, k] = jnp.zeros((2, 8, 128), F32)
     mt[z, k, 0, :, 0:16] = ids_ref[...].astype(F32)
     mt[z, k, 1, :, 0:16] = rw_ref[...]
 
-    def mt_copy(offset):
-        return remote(mt.at[z, k], mt.at[z, k], *pair("mt", offset), me.at_z(offset))
-
-    def mt_pass(offset, core=k):
-        at = mt.at[(z + offset) % 8, core]
-        return remote(at, at, *pair("mtp", offset), partner)
-
     for offset in range(1, 8):
-        start(mt_copy(offset))
-    start(mt_pass(0))
+        post(remote(mt.at[z, k], mt.at[z, k], *shares("mt", 0, 0), me.at_z(offset)))
+    shared.append((mt.at[pl.ds(0, 7), 0], "mt", 0))
+
+    def mt_pass(core):
+        return remote(mt.at[:, core], mt.at[:, core], *pair("one", 4), partner)
 
     wb = r["wb"]
     wb[k, z] = w_ref[:, pl.ds(pl.multiple_of(k * 128, 128), 128)]
@@ -262,6 +271,7 @@
     remote(give, wb.at[1 - k, z], *pair("one", 2), partner).wait_recv()
     for q in range(2, 4):
         ring_start(w_block(q), "w", q)
+    shared.append((wb.at[:, pl.ds(0, 7)], "w", 0))
 
     bias = r["bias"]
     own_place = order_ref[me.ctx]
@@ -272,26 +282,30 @@
     loads[0].wait()
     scaled(r["raw_g"], gs_ref, r["deq_g"])
     for offset in (1, 7, 2, 6, 3, 5, 4):
-        came = kv_at(8 - offset, 0)
-        remote(came, came, *pair("kv", offset), partner).wait_recv()
-        start(kv_across(8 - offset))
-        start(kv_pass(8 - offset, 0))
+        arrived(kv_at(8 - offset, 0), "kv", offset)
+        post(kv_across(8 - offset))
+    start(kv_pass(0))
     w_step(1)
-    for offset in range(1, 8):
-        came = mt.at[(z + 8 - offset) % 8, k]
-        remote(came, came, *pair("mt", offset), partner).wait_recv()
-        start(mt_pass(8 - offset))
-    for offset in (0, 7, 1, 6, 2, 5, 3, 4):
-        came = kv_at(offset, 1)
-        remote(came, came, *pair("kva", offset), partner).wait_recv()
-        start(kv_pass(offset, 1))
+    arrived(mt.at[pl.ds(0, 7), k], "mt", 0)
+    start(mt_pass(k))
+    arrived(kv_side(1, k), "kva", 0)
+    start(kv_pass(1))
+    w_step(2, range(2))
     for side in range(2):
-        for offset in range(8):
-            came = kv_at(offset, side, 1 - k)
-            remote(came, came, *pair("kvp", side, offset), partner).wait_recv()
+        remote(kv_side(side, 1 - k), kv_side(side, 1 - k), *pair("kvp", side), partner).wait_recv()
 
     ab = r["ab"]
     keys, values = kv[0].reshape(2048, 128), kv[1].reshape(2048, 128)
+    over = me.at_plane(0, 1)[0]
+
+    def a_part(core, side, n):
+        return ab.at[core, yh if side == 0 else 1 - yh, :, pl.ds(n * 256, 256)]
+
+    def a_start(n):
+        own = a_part(k, 0, n)
+        start(remote(own, own, *pair("a", n * 3 + 1), over))
+        start(remote(own, own, *pair("a", n * 3), partner))
+
     for h in range(4):
         to = slice(h * 128, (h + 1) * 128)
         scores = contract_last(q_ref[:, to], keys) * (1.0 / math.sqrt(HEAD_SIZE) * math.log2(math.e))
@@ -299,15 +313,14 @@
         exps = jnp.exp2(scores - jnp.max(scores, axis=1, keepdims=True))
         total = jnp.sum(exps, axis=1, keepdims=True)
         ab[k, yh, :, to] = (mul(exps.astype(BF16), values) / total).astype(BF16)
-        if h == 1:
-            w_step(2, range(2))
-    w_step(2, range(2, 4))
-    over = me.at_plane(0, 1)[0]
-    start(remote(ab.at[k, yh], ab.at[k, yh], *pair("a", 0), partner))
-    start(remote(ab.at[k, yh], ab.at[k, yh], *pair("a", 1), over))
-
-    for offset in range(8):
-        mt_pass(offset, 1 - k).wait_recv()
+        if h == 0:
+            w_step(2, range(2, 4))
+        if h == 2:
+            w_step(3, range(2))
+        if h % 2 == 1:
+            a_start(h // 2)
+    w_step(3, range(2, 4))
+    mt_pass(1 - k).wait_recv()
     tables = r["tables"]
     for n in range(16):
         for kind in range(2):
@@ -335,29 +348,17 @@
     weights_hi[...] = weights.astype(BF16)
     weights_lo[...] = (weights - weights.astype(BF16).astype(F32)).astype(BF16)
 
-    w_step(3)
-    came = ab.at[k, 1 - yh]
-    remote(came, came, *pair("a", 1), over).wait_recv()
-    start(remote(came, came, *pair("a", 2), partner))
-    for i, there in ((0, yh), (2, 1 - yh)):
-        came = ab.at[1 - k, there]
-        remote(came, came, *pair("a", i), partner).wait_recv()
-
-    px, rx, tot, yo, yi = r["px"], r["rx"], r["tot"], r["yo"], r["yi"]
+    for n in range(2):
+        came = a_part(k, 1, n)
+        remote(came, came, *pair("a", n * 3 + 1), over).wait_recv()
+        start(remote(came, came, *pair("a", n * 3 + 2), partner))
+    for n in range(2):
+        for i in (0, 2):
+            came = a_part(1 - k, i // 2, n)
+            remote(came, came, *pair("a", n * 3 + i), partner).wait_recv()
+
+    px, rx = r["px"], r["rx"]
     attended = [ab[core].reshape(256, 512) for core in range(2)]
-
-    def x_copy(g, dx):
-        lo, hi = GROUPS[g]
-        part = pl.ds(lo, hi - lo)
-        return remote(
-            px.at[(x + dx) % 4, part], rx.at[dx, part], *pair("x", g, dx), me.at_plane(dx, 0)[0]
-        )
-
-    def y_copy(g):
-        lo, hi = GROUPS[g]
-        part = pl.ds(lo, hi - lo)
-        return remote(yo.at[part], yi.at[part], *pair("y", g), over)
-
     for g, (lo, hi) in enumerate(GROUPS):
         if g == len(GROUPS) - 1:
             loads[1].wait()
@@ -367,35 +368,29 @@
             at = (z + OFFSETS[n]) % 8
             part = mul(attended[0], wb[0, at]) + mul(attended[1], wb[1, at])
             part = part.astype(BF16).reshape(2, 4, 32, 128)
-            for to in range(4):
-                px[to, n] = part[:, to]
-        for dx in range(1, 4):
-            start(x_copy(g, dx))
-
-    def place_columns(n, side, values):
-        at = pl.ds(pl.multiple_of((side * 8 + (z + OFFSETS[n]) % 8) * 128, 128), 128)
-        st[:, at] = values
-
-    for g, (lo, hi) in enumerate(GROUPS):
-        for dx in range(1, 4):
-            x_copy(g, dx).wait_recv()
-        for n in range(lo, hi):
-            total = px[x, n].astype(F32)
-            for dx in range(1, 4):
-                total = total + rx[dx, n].astype(F32)
-            tot[n] = total
-            yo[n] = tot[n, 1 - yh].astype(BF16)
-            place_columns(n, yh, tot[n, yh])
-        start(y_copy(g))
+            for side in range(2):
+                for to in range(4):
+                    px[side * 4 + to, n] = part[side, to]
+        cut = pl.ds(lo, hi - lo)
+        for d in range(1, 8):
+            device, there = me.at_plane(*PLANE[d])
+            post(remote(px.at[there, cut], rx.at[d, cut], *pair("x", g), device))
+        shared.append((rx.at[pl.ds(1, 7), cut], "x", g))
+
     remote(res_give, res.at[1 - k], *pair("one", 3), partner).wait_recv()
     for g, (lo, hi) in enumerate(GROUPS):
-        y_copy(g).wait_recv()
+        arrived(rx.at[pl.ds(1, 7), pl.ds(lo, hi - lo)], "x", g)
         for n in range(lo, hi):
-            place_columns(n, 1 - yh, yi[n].astype(F32))
+            for side in range(2):
+                total = (px[me.plane, n] if side == 0 else rx[4, n]).astype(F32)
+                for dx in range(1, 4):
+                    total = total + rx[side * 4 + dx, n].astype(F32)
+                at = ((yh if side == 0 else 1 - yh) * 8 + (z + OFFSETS[n]) % 8) * 128
+                st[:, pl.ds(pl.multiple_of(at, 128), 128)] = total
     st[...] = st[...] + res[...].reshape(32, 2048).astype(F32)
     squares = jnp.sum(st[...] * st[...], axis=1, keepdims=True)
     r["sq"][0] = jnp.broadcast_to(squares, (32, 128))
-    swap = remote(r["sq"].at[0], r["sq"].at[1], *pair("one", 4), partner)
+    swap = remote(r["sq"].at[0], r["sq"].at[1], *pair("one", 5), partner)
     start(swap)
     swap.wait_recv()
     mean = (r["sq"][0, :, 0:1] + r["sq"][1, :, 0:1]) / 4096.0
@@ -406,40 +401,40 @@
 
     def z_copy(q, source, to):
         block = xg.at[q, (z + source) % 8]
-        return remote(block, block, *pair("z", q, (source - to) % 8), me.at_z(to % 8))
-
-    def z_wait(q, source):
-        block = xg.at[q, (z + source) % 8]
-        remote(block, block, *pair("z", q, source), partner).wait_recv()
+        offset = (source - to) % 8
+        sems = shares("z", q, q * 3 + {2: 1, 6: 2}.get(offset, 0))
+        return remote(block, block, *sems, me.at_z(to % 8))
 
     def z_first(q):
         for to in (2, -2, 1, -1):
-            start(z_copy(q, 0, to))
+            post(z_copy(q, 0, to))
+        shared.append((xg.at[q, pl.ds(0, 7)], "z", q))
 
     def z_second(q):
         for side in (1, -1):
-            z_wait(q, (-2 * side) % 8)
-            start(z_copy(q, -2 * side, side))
+            arrived(xg.at[q, (z + 8 - 2 * side) % 8], "z", q * 3 + (2 if side == 1 else 1))
+            post(z_copy(q, -2 * side, side))
             if (side == 1) == (q % 2 == 0):
-                start(z_copy(q, -2 * side, 2 * side))
+                post(z_copy(q, -2 * side, 2 * side))
 
     def to_plane(bufs, bufr, name, q, d):
         device, there = me.at_plane(*PLANE[d])
-        return remote(bufs.at[q, there], bufr.at[q, me.plane], *pair(name, q, d), device)
-
-    def from_plane(bufr, name, q, d):
-        came = me.plane_from(*PLANE[d])
-        remote(bufr.at[q, came], bufr.at[q, came], *pair(name, q, d), partner).wait_recv()
-        return came
+        return remote(bufs.at[q, there], bufr.at[q, me.plane], *pair(name, q), device)
+
+    def plane_start(bufs, bufr, name, q):
+        for d in range(1, 8):
+            post(to_plane(bufs, bufr, name, q, d))
+        shared.append((bufs.at[q, pl.ds(0, 7)], name, q))
+        bufr[q, me.plane] = bufs[q, me.plane]
+
+    def plane_end(bufr, name, q):
+        arrived(bufr.at[q, pl.ds(0, 7)], name, q)
 
     ys, yr, xo = r["ys"], r["yr"], r["xo"]
     def pick(q):
         picked = contract_first(select[...], xg[q].reshape(256, ch)).astype(BF16)
         ys[q] = picked.reshape(8, 48, ch)
-        for d in range(1, 8):
-            start(to_plane(ys, yr, "pd", q, d))
-        yr[q, me.plane] = ys[q, me.plane]
-        start(remote(yr.at[q, me.plane], xo.at[q, me.plane], *pair("fw", q, 0), partner))
+        plane_start(ys, yr, "pd", q)
 
     ahead = 2
     for q in range(min(ahead, NQ)):
@@ -453,20 +448,17 @@
             if turn + ahead < NQ:
                 z_first(turn + ahead)
         if turn:
-            for source in (1, 7, 3, 5, 4):
-                z_wait(turn - 1, source)
+            arrived(xg.at[turn - 1, pl.ds(0, 5)], "z", (turn - 1) * 3)
             pick(turn - 1)
     start(remote(r["deq_d"].at[1], r["down_in"], *pair("one", 0), partner))
 
     gate = jnp.zeros((384, 384), F32)
     up = jnp.zeros((384, 384), F32)
     for q in range(NQ):
-        for d in range(1, 8):
-            came = from_plane(yr, "pd", q, d)
-            start(remote(yr.at[q, came], xo.at[q, came], *pair("fw", q, d), partner))
-        for d in range(8):
-            came = me.plane_from(*PLANE[d])
-            remote(yr.at[q, came], xo.at[q, came], *pair("fw", q, d), partner).wait_recv()
+        plane_end(yr, "pd", q)
+        swap = remote(yr.at[q], xo.at[q], *pair("fw", q), partner)
+        start(swap)
+        swap.wait_recv()
         for half, rows in ((0, yr), (1, xo)):
             block = rows[q].reshape(384, ch)
             gate = gate + mul(block, r["deq_g"][half, q * ch : (q + 1) * ch, :])
@@ -483,38 +475,45 @@
         cols = slice(q * ch, (q + 1) * ch)
         result = mul(hid[...], r["deq_d"][0, :, cols]) + mul(hid_in[...], r["down_in"][:, cols])
         es[q] = result.astype(BF16).reshape(8, 48, ch)
-        for d in range(1, 8):
-            start(to_plane(es, er, "ps", q, d))
-        er[q, me.plane] = es[q, me.plane]
+        plane_start(es, er, "ps", q)
 
     comb = r["comb"]
 
     towards = {1: 1, 7: -1, 3: 1, 5: -1, 2: 2, 6: -2}
     back_out, back_in = r["back_out"], r["back_in"]
 
-    def back(q, offset):
+    def back_kind(q, offset):
+        if offset in (3, 5):
+            return q * 3 + (1 if offset == 3 else 2)
+        if offset == 4:
+            return q * 3 + (1 if q % 2 == 0 else 2)
+        return q * 3
+
+    def back_slot(q, offset):
+        return {3: 0, 5: 2, 4: 1, 1: 3, 7: 4, 2: 5, 6: 6}[offset]
+
+    def back_start(q, offset, came=None):
+        part = comb[q, (z + offset) % 8]
+        if came is not None:
+            lo, count = came
+            arrived(back_in.at[q, pl.ds(lo, count)], "b", back_kind(q, 3 if offset == 2 else 5))
+            for n in range(lo, lo + count):
+                part = part + back_in[q, n].astype(F32)
+        slot = back_slot(q, offset)
+        back_out[q, slot] = part.astype(BF16)
         to = towards.get(offset, 2 if q % 2 == 0 else -2)
-        return remote(
-            back_out.at[q, offset], back_in.at[q, offset], *pair("b", q, offset), me.at_z(to % 8)
-        )
-
-    def back_start(q, offset, came=()):
-        part = comb[q, (z + offset) % 8]
-        for other in came:
-            back(q, other).wait_recv()
-            part = part + back_in[q, other].astype(F32)
-        back_out[q, offset] = part.astype(BF16)
-        start(back(q, offset))
+        sems = shares("b", q, back_kind(q, offset))
+        post(remote(back_out.at[q, slot], back_in.at[q, slot], *sems, me.at_z(to % 8)))
 
     def back_second(q):
-        back_start(q, 2, (3, 4) if q % 2 == 0 else (3,))
-        back_start(q, 6, (5,) if q % 2 == 0 else (5, 4))
+        back_start(q, 2, (0, 2) if q % 2 == 0 else (0, 1))
+        back_start(q, 6, (2, 1) if q % 2 == 0 else (1, 2))
+        shared.append((back_out.at[q, pl.ds(0, 7)], "b", q))
 
     fin, fin_in = r["fin"], r["fin_in"]
     for turn in range(NQ + 1):
         if turn < NQ:
-            for d in range(1, 8):
-                from_plane(er, "ps", turn, d)
+            plane_end(er, "ps", turn)
             rows = er[turn].reshape(384, ch)
             total = mul(weights_hi[...], rows) + mul(weights_lo[...], rows)
             comb[turn] = total.reshape(8, 32, ch)
@@ -524,9 +523,9 @@
             back_second(turn - 1)
     for q in range(NQ):
         total = comb[q, z] + st[:, q * ch : (q + 1) * ch]
-        for offset in (1, 7, 2, 6):
-            back(q, offset).wait_recv()
-            total = total + back_in[q, offset].astype(F32)
+        arrived(back_in.at[q, pl.ds(3, 4)], "b", q * 3)
+        for n in range(3, 7):
+            total = total + back_in[q, n].astype(F32)
         fin[q] = total.astype(BF16).reshape(2, 16, ch)
         start(remote(fin.at[q, 1 - k], fin_in.at[q], *pair("fn", q), partner))
     for q in range(NQ):
@@ -539,6 +538,8 @@
             out_ref[:, pl.ds(pl.multiple_of(at + (1 - k) * 128, 128), 128)] = got[:, piece]
     for copy in sends:
         copy.wait_send()
+    for buf, name, send in shared:
+        remote(buf, buf, *shares(name, send, 0), partner).wait_send()
 
 
 def scratch():
@@ -551,11 +552,8 @@
         "gain": ((1, 2048), F32),
         "bias": ((128, 2048), F32),
         "ab": ((2, 2, 128, 512), BF16),
-        "px": ((4, 8, 2, 32, 128), BF16),
-        "rx": ((4, 8, 2, 32, 128), BF16),
-        "tot": ((8, 2, 32, 128), F32),
-        "yo": ((8, 32, 128), BF16),
-        "yi": ((8, 32, 128), BF16),
+        "px": ((8, 8, 32, 128), BF16),
+        "rx": ((8, 8, 32, 128), BF16),
         "st": ((32, 2048), F32),
         "sq": ((2, 32, 128), F32),
         "mt": ((8, 2, 2, 8, 128), F32),
@@ -587,27 +585,24 @@
     made = {name: pltpu.VMEM(*what) for name, what in shapes.items()}
     made["w_sem"] = pltpu.SemaphoreType.DMA((3,))
     copies = {
-        "kv": (8,),
-        "kva": (8,),
-        "kvp": (2, 8),
-        "mt": (8,),
-        "mtp": (8,),
-        "one": (6,),
-        "wr": (4, 4),
-        "wl": (4, 4),
-        "a": (3,),
-        "x": (len(GROUPS), 4),
-        "y": (len(GROUPS),),
-        "z": (NQ, 8),
-        "pd": (NQ, 8),
-        "fw": (NQ, 8),
-        "ps": (NQ, 8),
-        "b": (NQ, 8),
-        "fn": (NQ,),
+        "kv": (1, 8),
+        "kva": (1, 1),
+        "kvp": (2, 2),
+        "mt": (1, 1),
+        "one": (7, 7),
+        "w": (1, 32),
+        "a": (6, 6),
+        "x": (len(GROUPS), len(GROUPS)),
+        "z": (NQ, 3 * NQ),
+        "pd": (NQ, NQ),
+        "fw": (NQ, NQ),
+        "ps": (NQ, NQ),
+        "b": (NQ, 3 * NQ),
+        "fn": (NQ, NQ),
     }
-    for name, shape in copies.items():
-        made[name + "_s"] = pltpu.SemaphoreType.DMA(shape)
-        made[name + "_r"] = pltpu.SemaphoreType.DMA(shape)
+    for name, (sent, received) in copies.items():
+        made[name + "_s"] = pltpu.SemaphoreType.DMA((sent,))
+        made[name + "_r"] = pltpu.SemaphoreType.DMA((received,))
     return made
 
 

time: 124 us -> 120 us (0.968)
  Pallas kernels: 122 us -> 118 us
    pallas_call x1, Pallas kernels: 122 us -> 118 us  [layer(): pl.pallas_call(layer_kernel, out_shape=jax.ShapeDtypeStruct((16, 4096), B...]
where the time goes in v5:
time: 120 us
  Pallas kernels  118 us (98%)
  local copies, waits for them, and re-layouts  1.57 us (1%)
    pallas_call x1, Pallas kernels, layer(): pl.pallas_call(layer_kernel, out_shape=jax.ShapeDtypeStruct((16, 4096), B...  118 us

profile of v5, /device:TPU:1, one launch (start us, length us, event | category | flops | bytes accessed | tf_op | source)
XLA Modules:
  0.0 119.7 jit_solution(6563707096219772168)
XLA Ops:
  0.0 118.1 %layer.1 = bf16[16,4096]{1,0:T(8,128)(2,1)} custom-call(bf16[128,512]{1,0:T(8,128)(2,1)} %q_ref.1, bf16[128,512]{1,0:T(8,128)(2,1)} %kq_ref.1, bf16[128,512]{1,0:T(8,128)(2,1)} %vq_ref.1, s32[2,4]{1,0:T(2,128)} %ke_ref.1, s32[2,4]{1,0:T(2,128)} %ve_ref.1, s32[16]{0:T(128)} %order_ref.1, bf16[512,256]{1,0:T(8,128)(2,1)} %w_ref.1, bf16[16,4096]{1,0:T(8,128)(2,1)} %res_ref.1, ...), custom_call_target="tpu_custom_call" | custom-call | tf_op jit(solution)/shard_map/layer/pallas_call | solution.py:616
  118.1 1.6 %copy.19 = bf16[16,4096]{1,0:T(8,128)(2,1)} copy(bf16[16,4096]{1,0:T(8,128)(2,1)} %layer.1) | data formatting | bytes 262144

commit v6 on v5

--- a/solution.py
+++ b/solution.py
@@ -15,11 +15,8 @@
 NQ = 4
 OFFSETS = (0, 1, 7, 2, 6, 3, 5, 4)
 GROUPS = ((0, 3), (3, 5), (5, 8))
+SLOTS = ((0, 1), (1, 2))
 PLANE = [(dx, dy) for dy in range(2) for dx in range(4)]
-
-
-def contract_first(lhs, rhs):
-    return lax.dot_general(lhs, rhs, (((0,), (0,)), ((), ())), preferred_element_type=F32)
 
 
 def contract_last(lhs, rhs):
@@ -72,6 +69,9 @@
 
     def plane_from(self, dx, dy):
         return ((self.yh + 2 - dy) % 2) * 4 + (self.x + 4 - dx) % 4
+
+    def other_part(self):
+        return {"ctx": self.ctx, "exp": self.exp, "dp": 1 - self.dp}
 
     def other_core(self):
         return {"ctx": self.ctx, "exp": self.x * 2 + (1 - self.k), "dp": self.dp}
@@ -137,14 +137,14 @@
 
     barrier = pltpu.get_barrier_semaphore()
     peers = [me.at_plane(dx, dy)[0] for dx, dy in PLANE[1:]]
-    peers = peers + [partner, me.at_ctx(8)] + [me.at_z(i) for i in range(1, 8)]
+    peers = peers + [partner, me.at_ctx(8), me.other_part()] + [me.at_z(i) for i in range(1, 8)]
     for peer in peers:
         pl.semaphore_signal(barrier, inc=1, device_id=peer, device_id_type=MESH)
     pl.semaphore_wait(barrier, len(peers))
 
     def gather(buf, name, q, step, rightward):
         block = (z + 8 - step) % 8 if rightward else (z + step) % 8
-        sems = shares(name, 0, q * 8 + step * 2 + (0 if rightward else 1))
+        sems = shares(name, q, q * 8 + step * 2 + (0 if rightward else 1))
         return remote(buf(block), buf(block), *sems, right if rightward else left)
 
     def gathered(buf, name, q, step, rightward):
@@ -216,12 +216,19 @@
 
     def w_block(q):
         core = k if q < 2 else 1 - k
-        rows = pl.ds((q % 2) * 256, 256)
+        rows = pl.ds(q * 256 if q < 2 else pl.multiple_of(me.dp * 256, 256), 256)
         return lambda block: wb.at[core, block, rows]
 
-    def w_step(step, parts=range(4)):
+    def w_step(step, parts=range(3)):
         for q in parts:
             ring_step(w_block(q), "w", q, step)
+            if q == 2:
+                for offset in (8 - step, step) if step < 4 else (4,):
+                    block = w_block(2)((z + offset) % 8)
+                    post(remote(block, block, *shares("ws", 0, step), me.other_part()))
+
+    def w_shared(step):
+        arrived(wb.at[0, pl.ds(0, 2 if step < 4 else 1), pl.ds(0, 256)], "ws", step)
 
     start(remote(give, wb.at[k, z], *pair("one", 2), partner))
     for q in range(2):
@@ -269,9 +276,10 @@
         lax.fori_loop(lo, hi, body, 0)
 
     remote(give, wb.at[1 - k, z], *pair("one", 2), partner).wait_recv()
-    for q in range(2, 4):
-        ring_start(w_block(q), "w", q)
-    shared.append((wb.at[:, pl.ds(0, 7)], "w", 0))
+    ring_start(w_block(2), "w", 2)
+    for q in range(3):
+        shared.append((wb.at[0, pl.ds(0, 7), pl.ds(0, 256)], "w", q))
+    shared.append((wb.at[0, pl.ds(0, 7), pl.ds(0, 256)], "ws", 0))
 
     bias = r["bias"]
     own_place = order_ref[me.ctx]
@@ -314,12 +322,12 @@
         total = jnp.sum(exps, axis=1, keepdims=True)
         ab[k, yh, :, to] = (mul(exps.astype(BF16), values) / total).astype(BF16)
         if h == 0:
-            w_step(2, range(2, 4))
+            w_step(2, range(2, 3))
         if h == 2:
             w_step(3, range(2))
         if h % 2 == 1:
             a_start(h // 2)
-    w_step(3, range(2, 4))
+    w_step(3, range(2, 3))
     mt_pass(1 - k).wait_recv()
     tables = r["tables"]
     for n in range(16):
@@ -341,10 +349,10 @@
     second = lax.broadcasted_iota(jnp.int32, (256, 256), 1)
     earlier = (second < first) & (second // 16 == first // 16)
     number = mul(jnp.where(earlier, 1.0, 0.0).astype(BF16), member.astype(BF16))
-    here = (number == (slot % 3).astype(F32)) & ((slot % 48) // 3 == token // 16)
+    here = (number == (slot % 48 // 16).astype(F32)) & (slot % 16 == token // 16)
     weights = jnp.where(here, weights, 0.0)
     select, weights_hi, weights_lo = r["sel"], r["whi"], r["wlo"]
-    select[...] = jnp.where(here, member, 0.0).astype(BF16)
+    select[...] = jnp.transpose(jnp.where(here, member, 0.0)).astype(BF16)
     weights_hi[...] = weights.astype(BF16)
     weights_lo[...] = (weights - weights.astype(BF16).astype(F32)).astype(BF16)
 
@@ -364,6 +372,8 @@
             loads[1].wait()
             scaled(r["raw_u"], us_ref, r["deq_u"])
             w_step(4)
+        for step in ((1,), (2,), (3, 4))[g]:
+            w_shared(step)
         for n in range(lo, hi):
             at = (z + OFFSETS[n]) % 8
             part = mul(attended[0], wb[0, at]) + mul(attended[1], wb[1, at])
@@ -417,24 +427,29 @@
             if (side == 1) == (q % 2 == 0):
                 post(z_copy(q, -2 * side, 2 * side))
 
-    def to_plane(bufs, bufr, name, q, d):
-        device, there = me.at_plane(*PLANE[d])
-        return remote(bufs.at[q, there], bufr.at[q, me.plane], *pair(name, q), device)
-
-    def plane_start(bufs, bufr, name, q):
+    def plane_start(bufs, bufr, name, q, g):
+        slots = pl.ds(*SLOTS[g])
         for d in range(1, 8):
-            post(to_plane(bufs, bufr, name, q, d))
-        shared.append((bufs.at[q, pl.ds(0, 7)], name, q))
-        bufr[q, me.plane] = bufs[q, me.plane]
-
-    def plane_end(bufr, name, q):
-        arrived(bufr.at[q, pl.ds(0, 7)], name, q)
+            device, there = me.at_plane(*PLANE[d])
+            src, dst = bufs.at[q, there, slots], bufr.at[q, me.plane, slots]
+            post(remote(src, dst, *pair(name, q * 2 + g), device))
+        shared.append((bufs.at[q, pl.ds(0, 7), slots], name, q * 2 + g))
+
+    def plane_end(bufr, name, q, g):
+        arrived(bufr.at[q, pl.ds(0, 7), pl.ds(*SLOTS[g])], name, q * 2 + g)
 
     ys, yr, xo = r["ys"], r["yr"], r["xo"]
+
     def pick(q):
-        picked = contract_first(select[...], xg[q].reshape(256, ch)).astype(BF16)
-        ys[q] = picked.reshape(8, 48, ch)
-        plane_start(ys, yr, "pd", q)
+        picked = mul(select[...], xg[q].reshape(256, ch)).astype(BF16)
+        ys[q] = picked.reshape(8, 3, 16, ch)
+        plane_start(ys, yr, "pd", q, 0)
+        if q < NQ // 2:
+            plane_start(ys, yr, "pd", q, 1)
+        if q == NQ - 1:
+            for late in range(NQ // 2, NQ):
+                plane_start(ys, yr, "pd", late, 1)
+        yr[q, me.plane] = ys[q, me.plane]
 
     ahead = 2
     for q in range(min(ahead, NQ)):
@@ -452,30 +467,56 @@
             pick(turn - 1)
     start(remote(r["deq_d"].at[1], r["down_in"], *pair("one", 0), partner))
 
-    gate = jnp.zeros((384, 384), F32)
-    up = jnp.zeros((384, 384), F32)
-    for q in range(NQ):
-        plane_end(yr, "pd", q)
-        swap = remote(yr.at[q], xo.at[q], *pair("fw", q), partner)
+    es, er = r["es"], r["er"]
+
+    def swap_rows(q, g):
+        slots = pl.ds(*SLOTS[g])
+        return remote(yr.at[q, :, slots], xo.at[q, :, slots], *pair("fw", q * 2 + g), partner)
+
+    def swap_start(q, g):
+        plane_end(yr, "pd", q, g)
+        start(swap_rows(q, g))
+
+    def hidden(g):
+        lo, count = SLOTS[g]
+        rows = 128 * count
+        gate = jnp.zeros((rows, 384), F32)
+        up = jnp.zeros((rows, 384), F32)
+        for q in range(0 if g == 0 else NQ // 2, NQ - 1):
+            swap_start(q, g)
+        for q in range(NQ):
+            if q == NQ - 1:
+                swap_start(q, g)
+                for early in range(NQ // 2 if g == 0 else 0):
+                    swap_start(early, 1)
+            swap_rows(q, g).wait_recv()
+            cols = slice(q * ch, (q + 1) * ch)
+            for half, buf in ((0, yr), (1, xo)):
+                block = buf[q, :, lo : lo + count].reshape(rows, ch)
+                gate = gate + mul(block, r["deq_g"][half, cols, :])
+                up = up + mul(block, r["deq_u"][half, cols, :])
+        r["hid%d" % g][...] = (gate / (1.0 + jnp.exp(-gate)) * up).astype(BF16)
+
+    def results(g):
+        lo, count = SLOTS[g]
+        mine, came = r["hid%d" % g], r["hid_in%d" % g]
+        swap = remote(mine, came, *pair("one", 1 + 5 * g), partner)
         start(swap)
+        if g == 0:
+            remote(r["deq_d"].at[1], r["down_in"], *pair("one", 0), partner).wait_recv()
+        ahead = mul(mine[...], r["deq_d"][0, :, 0:ch])
         swap.wait_recv()
-        for half, rows in ((0, yr), (1, xo)):
-            block = rows[q].reshape(384, ch)
-            gate = gate + mul(block, r["deq_g"][half, q * ch : (q + 1) * ch, :])
-            up = up + mul(block, r["deq_u"][half, q * ch : (q + 1) * ch, :])
-    hid, hid_in = r["hid"], r["hid_in"]
-    hid[...] = (gate / (1.0 + jnp.exp(-gate)) * up).astype(BF16)
-    swap = remote(hid, hid_in, *pair("one", 1), partner)
-    start(swap)
-    remote(r["deq_d"].at[1], r["down_in"], *pair("one", 0), partner).wait_recv()
-    swap.wait_recv()
-
-    es, er = r["es"], r["er"]
-    for q in range(NQ):
-        cols = slice(q * ch, (q + 1) * ch)
-        result = mul(hid[...], r["deq_d"][0, :, cols]) + mul(hid_in[...], r["down_in"][:, cols])
-        es[q] = result.astype(BF16).reshape(8, 48, ch)
-        plane_start(es, er, "ps", q)
+        for q in range(NQ):
+            cols = slice(q * ch, (q + 1) * ch)
+            result = ahead if q == 0 else mul(mine[...], r["deq_d"][0, :, cols])
+            result = result + mul(came[...], r["down_in"][:, cols])
+            es[q, :, lo : lo + count] = result.astype(BF16).reshape(8, count, 16, ch)
+            plane_start(es, er, "ps", q, g)
+            er[q, me.plane, lo : lo + count] = es[q, me.plane, lo : lo + count]
+
+    for g in range(2):
+        hidden(g)
+        results(g)
 
     comb = r["comb"]
 
@@ -513,7 +554,8 @@
     fin, fin_in = r["fin"], r["fin_in"]
     for turn in range(NQ + 1):
         if turn < NQ:
-            plane_end(er, "ps", turn)
+            for g in range(2):
+                plane_end(er, "ps", turn, g)
             rows = er[turn].reshape(384, ch)
             total = mul(weights_hi[...], rows) + mul(weights_lo[...], rows)
             comb[turn] = total.reshape(8, 32, ch)
@@ -558,13 +600,13 @@
         "sq": ((2, 32, 128), F32),
         "mt": ((8, 2, 2, 8, 128), F32),
         "tables": ((2, 256, 128), F32),
-        "sel": ((256, 384), BF16),
+        "sel": ((384, 256), BF16),
         "whi": ((256, 384), BF16),
         "wlo": ((256, 384), BF16),
         "xg": ((NQ, 8, 32, ch), BF16),
-        "ys": ((NQ, 8, 48, ch), BF16),
-        "yr": ((NQ, 8, 48, ch), BF16),
-        "xo": ((NQ, 8, 48, ch), BF16),
+        "ys": ((NQ, 8, 3, 16, ch), BF16),
+        "yr": ((NQ, 8, 3, 16, ch), BF16),
+        "xo": ((NQ, 8, 3, 16, ch), BF16),
         "raw_g": ((4096, 384), BF16),
         "raw_u": ((4096, 384), BF16),
         "raw_d": ((384, 4096), BF16),
@@ -572,10 +614,12 @@
         "deq_u": ((2, 2048, 384), BF16),
         "deq_d": ((2, 384, 2048), BF16),
         "down_in": ((384, 2048), BF16),
-        "hid": ((384, 384), BF16),
-        "hid_in": ((384, 384), BF16),
-        "es": ((NQ, 8, 48, ch), BF16),
-        "er": ((NQ, 8, 48, ch), BF16),
+        "hid0": ((128, 384), BF16),
+        "hid_in0": ((128, 384), BF16),
+        "hid1": ((256, 384), BF16),
+        "hid_in1": ((256, 384), BF16),
+        "es": ((NQ, 8, 3, 16, ch), BF16),
+        "er": ((NQ, 8, 3, 16, ch), BF16),
         "comb": ((NQ, 8, 32, ch), F32),
         "back_out": ((NQ, 8, 32, ch), BF16),
         "back_in": ((NQ, 8, 32, ch), BF16),
@@ -590,13 +634,14 @@
         "kvp": (2, 2),
         "mt": (1, 1),
         "one": (7, 7),
-        "w": (1, 32),
+        "w": (3, 24),
+        "ws": (1, 5),
         "a": (6, 6),
         "x": (len(GROUPS), len(GROUPS)),
         "z": (NQ, 3 * NQ),
-        "pd": (NQ, NQ),
-        "fw": (NQ, NQ),
-        "ps": (NQ, NQ),
+        "pd": (2 * NQ, 2 * NQ),
+        "fw": (2 * NQ, 2 * NQ),
+        "ps": (2 * NQ, 2 * NQ),
         "b": (NQ, 3 * NQ),
         "fn": (NQ, NQ),
     }

time: 120 us -> 115 us (0.958)
  Pallas kernels: 118 us -> 113 us
    pallas_call x1, Pallas kernels: 118 us -> 113 us  [layer(): pl.pallas_call(layer_kernel, out_shape=jax.ShapeDtypeStruct((16, 4096), B...]
where the time goes in v6:
time: 115 us
  Pallas kernels  113 us (98%)
  local copies, waits for them, and re-layouts  1.57 us (1%)
    pallas_call x1, Pallas kernels, layer(): pl.pallas_call(layer_kernel, out_shape=jax.ShapeDtypeStruct((16, 4096), B...  113 us

profile of v6, /device:TPU:1, one launch (start us, length us, event | category | flops | bytes accessed | tf_op | source)
XLA Modules:
  0.0 114.7 jit_solution(17630509860508604326)
XLA Ops:
  0.0 113.1 %layer.1 = bf16[16,4096]{1,0:T(8,128)(2,1)} custom-call(bf16[128,512]{1,0:T(8,128)(2,1)} %q_ref.1, bf16[128,512]{1,0:T(8,128)(2,1)} %kq_ref.1, bf16[128,512]{1,0:T(8,128)(2,1)} %vq_ref.1, s32[2,4]{1,0:T(2,128)} %ke_ref.1, s32[2,4]{1,0:T(2,128)} %ve_ref.1, s32[16]{0:T(128)} %order_ref.1, bf16[512,256]{1,0:T(8,128)(2,1)} %w_ref.1, bf16[16,4096]{1,0:T(8,128)(2,1)} %res_ref.1, ...), custom_call_target="tpu_custom_call" | custom-call | tf_op jit(solution)/shard_map/layer/pallas_call | solution.py:661
  113.1 1.6 %copy.19 = bf16[16,4096]{1,0:T(8,128)(2,1)} copy(bf16[16,4096]{1,0:T(8,128)(2,1)} %layer.1) | data formatting | bytes 262144

commit v7 on v6

--- a/solution.py
+++ b/solution.py
@@ -296,14 +296,35 @@
     w_step(1)
     arrived(mt.at[pl.ds(0, 7), k], "mt", 0)
     start(mt_pass(k))
+    acc, top, norm = r["acc"], r["top"], r["norm"]
+
+    def kv_passed(side):
+        came = kv_side(side, 1 - k)
+        remote(came, came, *pair("kvp", side), partner).wait_recv()
+
+    def attend(h, side):
+        block = yh if side == 0 else 1 - yh
+        at = pl.ds(pl.multiple_of(block * 8, 8), 8)
+        keys, values = kv[0, at].reshape(1024, 128), kv[1, at].reshape(1024, 128)
+        scale = 1.0 / math.sqrt(HEAD_SIZE) * math.log2(math.e)
+        scores = contract_last(q_ref[:, h * 128 : (h + 1) * 128], keys) * scale
+        scores = scores + bias[:, pl.ds(pl.multiple_of(block * 1024, 1024), 1024)]
+        high = jnp.max(scores, axis=1, keepdims=True)
+        exps = jnp.exp2(scores - high)
+        return high, jnp.sum(exps, axis=1, keepdims=True), mul(exps.astype(BF16), values)
+
+    kv_passed(0)
+    for h in range(4):
+        high, total, mixed = attend(h, 0)
+        top[h] = jnp.broadcast_to(high, (128, 128))
+        norm[h] = jnp.broadcast_to(total, (128, 128))
+        acc[h] = mixed
     arrived(kv_side(1, k), "kva", 0)
     start(kv_pass(1))
     w_step(2, range(2))
-    for side in range(2):
-        remote(kv_side(side, 1 - k), kv_side(side, 1 - k), *pair("kvp", side), partner).wait_recv()
+    kv_passed(1)
 
     ab = r["ab"]
-    keys, values = kv[0].reshape(2048, 128), kv[1].reshape(2048, 128)
     over = me.at_plane(0, 1)[0]
 
     def a_part(core, side, n):
@@ -316,11 +337,11 @@
 
     for h in range(4):
         to = slice(h * 128, (h + 1) * 128)
-        scores = contract_last(q_ref[:, to], keys) * (1.0 / math.sqrt(HEAD_SIZE) * math.log2(math.e))
-        scores = scores + bias[...]
-        exps = jnp.exp2(scores - jnp.max(scores, axis=1, keepdims=True))
-        total = jnp.sum(exps, axis=1, keepdims=True)
-        ab[k, yh, :, to] = (mul(exps.astype(BF16), values) / total).astype(BF16)
+        high, total, mixed = attend(h, 1)
+        both = jnp.maximum(top[h], high)
+        old, new = jnp.exp2(top[h] - both), jnp.exp2(high - both)
+        total = norm[h] * old + total * new
+        ab[k, yh, :, to] = ((acc[h] * old + mixed * new) / total).astype(BF16)
         if h == 0:
             w_step(2, range(2, 3))
         if h == 2:
@@ -593,6 +614,9 @@
         "res_give": ((16, 2048), BF16),
         "gain": ((1, 2048), F32),
         "bias": ((128, 2048), F32),
+        "acc": ((4, 128, 128), F32),
+        "top": ((4, 128, 128), F32),
+        "norm": ((4, 128, 128), F32),
         "ab": ((2, 2, 128, 512), BF16),
         "px": ((8, 8, 32, 128), BF16),
         "rx": ((8, 8, 32, 128), BF16),

time: 115 us -> 115 us (level)
  no operation moved by 1% of the time
where the time goes in v7:
time: 115 us; the launch traced here: 114 us
  Pallas kernels  113 us (98%)
  local copies, waits for them, and re-layouts  1.57 us (1%)
    pallas_call x1, Pallas kernels, layer(): pl.pallas_call(layer_kernel, out_shape=jax.ShapeDtypeStruct((16, 4096), B...  113 us

profile of v7, /device:TPU:1, one launch (start us, length us, event | category | flops | bytes accessed | tf_op | source)
XLA Modules:
  0.0 114.4 jit_solution(11953581856545894020)
XLA Ops:
  0.0 112.9 %layer.1 = bf16[16,4096]{1,0:T(8,128)(2,1)} custom-call(bf16[128,512]{1,0:T(8,128)(2,1)} %q_ref.1, bf16[128,512]{1,0:T(8,128)(2,1)} %kq_ref.1, bf16[128,512]{1,0:T(8,128)(2,1)} %vq_ref.1, s32[2,4]{1,0:T(2,128)} %ke_ref.1, s32[2,4]{1,0:T(2,128)} %ve_ref.1, s32[16]{0:T(128)} %order_ref.1, bf16[512,256]{1,0:T(8,128)(2,1)} %w_ref.1, bf16[16,4096]{1,0:T(8,128)(2,1)} %res_ref.1, ...), custom_call_target="tpu_custom_call" | custom-call | tf_op jit(solution)/shard_map/layer/pallas_call | solution.py:685
  112.9 1.6 %copy.19 = bf16[16,4096]{1,0:T(8,128)(2,1)} copy(bf16[16,4096]{1,0:T(8,128)(2,1)} %layer.1) | data formatting | bytes 262144

commit v8 on v6

--- a/solution.py
+++ b/solution.py
@@ -198,21 +198,10 @@
     shared.append((kv.at[0, pl.ds(0, 7)], "kv", 0))
     shared.append((kv.at[0, pl.ds(0, 8)], "kva", 0))
 
-    mt = r["mt"]
-    mt[z, k] = jnp.zeros((2, 8, 128), F32)
-    mt[z, k, 0, :, 0:16] = ids_ref[...].astype(F32)
-    mt[z, k, 1, :, 0:16] = rw_ref[...]
-
-    for offset in range(1, 8):
-        post(remote(mt.at[z, k], mt.at[z, k], *shares("mt", 0, 0), me.at_z(offset)))
-    shared.append((mt.at[pl.ds(0, 7), 0], "mt", 0))
-
-    def mt_pass(core):
-        return remote(mt.at[:, core], mt.at[:, core], *pair("one", 4), partner)
-
     wb = r["wb"]
+    give = w_ref.at[:, pl.ds(pl.multiple_of((1 - k) * 128, 128), 128)]
+    start(remote(give, wb.at[k, z], *pair("one", 2), partner))
     wb[k, z] = w_ref[:, pl.ds(pl.multiple_of(k * 128, 128), 128)]
-    give = w_ref.at[:, pl.ds(pl.multiple_of((1 - k) * 128, 128), 128)]
 
     def w_block(q):
         core = k if q < 2 else 1 - k
@@ -230,9 +219,20 @@
     def w_shared(step):
         arrived(wb.at[0, pl.ds(0, 2 if step < 4 else 1), pl.ds(0, 256)], "ws", step)
 
-    start(remote(give, wb.at[k, z], *pair("one", 2), partner))
     for q in range(2):
         ring_start(w_block(q), "w", q)
+
+    mt = r["mt"]
+    mt[z, k] = jnp.zeros((2, 8, 128), F32)
+    mt[z, k, 0, :, 0:16] = ids_ref[...].astype(F32)
+    mt[z, k, 1, :, 0:16] = rw_ref[...]
+
+    for offset in range(1, 8):
+        post(remote(mt.at[z, k], mt.at[z, k], *shares("mt", 0, 0), me.at_z(offset)))
+    shared.append((mt.at[pl.ds(0, 7), 0], "mt", 0))
+
+    def mt_pass(core):
+        return remote(mt.at[:, core], mt.at[:, core], *pair("one", 4), partner)
 
     res, res_give, gain = r["res"], r["res_give"], r["gain"]
     for c in range(16):

time: 115 us -> 115 us (level)
  no operation moved by 1% of the time
where the time goes in v8:
time: 115 us
  Pallas kernels  113 us (98%)
  local copies, waits for them, and re-layouts  1.57 us (1%)
    pallas_call x1, Pallas kernels, layer(): pl.pallas_call(layer_kernel, out_shape=jax.ShapeDtypeStruct((16, 4096), B...  113 us

profile of v8, /device:TPU:1, one launch (start us, length us, event | category | flops | bytes accessed | tf_op | source)
XLA Modules:
  0.0 114.5 jit_solution(8584386449836405708)
XLA Ops:
  0.0 112.9 %layer.1 = bf16[16,4096]{1,0:T(8,128)(2,1)} custom-call(bf16[128,512]{1,0:T(8,128)(2,1)} %q_ref.1, bf16[128,512]{1,0:T(8,128)(2,1)} %kq_ref.1, bf16[128,512]{1,0:T(8,128)(2,1)} %vq_ref.1, s32[2,4]{1,0:T(2,128)} %ke_ref.1, s32[2,4]{1,0:T(2,128)} %ve_ref.1, s32[16]{0:T(128)} %order_ref.1, bf16[512,256]{1,0:T(8,128)(2,1)} %w_ref.1, bf16[16,4096]{1,0:T(8,128)(2,1)} %res_ref.1, ...), custom_call_target="tpu_custom_call" | custom-call | tf_op jit(solution)/shard_map/layer/pallas_call | solution.py:661
  113.0 1.6 %copy.19 = bf16[16,4096]{1,0:T(8,128)(2,1)} copy(bf16[16,4096]{1,0:T(8,128)(2,1)} %layer.1) | data formatting | bytes 262144
